TPU v7x, 256 devices: a whole 4x4x8 slice. The times are simulated.
256 devices in a mesh: coarse: 8 (over x, core), sub: 32 (over y, z).
Axes of the slice: x: 4, y: 4, z: 8, core: 2. Of those that a mesh axis runs over, the one named last changes fastest.
Arguments:
- local_operators: bfloat16 [256, 2048, 2048], P(('coarse', 'sub')), as said below
- couplings: bfloat16 [256, 24, 2048], P(('coarse', 'sub')), may hold values from -0.125 to 0.125
- coarse_inverse: float32 [1536, 1536], P('coarse'), as said below
- local_loads: float32 [256, 128, 2048], P(('coarse', 'sub')), may hold values from -6 to 6
- face_lists: int32 [256, 4, 384], P(('coarse', 'sub')), may hold values from 0 to 2047, as said below
- face_counts: int32 [256, 4], P(('coarse', 'sub')), may hold values from 0 to 384, as said below
- corner_map: int32 [256, 24], P(('coarse', 'sub')), may hold values from 0 to 1535
Outputs:
- solution: float32 [256, 128, 2048], P(('coarse', 'sub'))
- residual: float32 [256, 128, 2048], P(('coarse', 'sub'))
Inputs may be any that keep to these rules, and one draw needn't show every extreme that they name: `local_operators`: each subdomain's matrix is symmetric and positive definite. `coarse_inverse`: symmetric and positive definite. `face_counts`: the 32 subdomains of one coarse index form a grid of 4 rows of 8; a face's count equals that of the neighbour's matching face and is 0 where the grid has no neighbour on that side; in every draw some face holds exactly 384. `face_lists`: all entries of one subdomain's four lists are distinct; the used slots of a face pair, slot by slot, with the same slots of the neighbour's matching face; slots past the count are to be ignored.
All inputs are finite; a program needn't handle non-finite values.
Results may differ from a plain program's by a relative error of at most 0.025.
Values sent between devices are 32-bit elements; how exact they have to be, the bound alone decides.
A program may use at most 128 MiB of HBM per device.

v0:
```python
import jax
import jax.numpy as jnp
from jax import lax
from jax.sharding import PartitionSpec as P

ITERS = 3


HIGH = lax.Precision.HIGHEST


def shifted(value, axis, steps):
    count = lax.axis_size(axis)
    first, last = (max(0, -steps), min(count, count - steps))
    return lax.ppermute(value, axis, [(source, source + steps) for source in range(first, last)])


def spd_solve(matrix, right):
    factor = jnp.linalg.cholesky(matrix)
    middle = lax.linalg.triangular_solve(factor, right, left_side=True, lower=True)
    return lax.linalg.triangular_solve(factor, middle, left_side=True, lower=True, transpose_a=True)


def split_product(rounded, values):
    upper = values.astype(jnp.bfloat16)
    remainder = values - upper.astype(jnp.float32)
    middle = remainder.astype(jnp.bfloat16)
    lowest = (remainder - middle.astype(jnp.float32)).astype(jnp.bfloat16)
    total = jnp.einsum("lm,km->lk", rounded, upper, preferred_element_type=jnp.float32)
    total = total + jnp.einsum("lm,km->lk", rounded, middle, preferred_element_type=jnp.float32)
    return total + jnp.einsum("lm,km->lk", rounded, lowest, preferred_element_type=jnp.float32)


def local(
    local_operators, couplings, coarse_inverse, local_loads, face_lists, face_counts, corner_map
):
    operator_block = local_operators[0]
    coupling = couplings[0]
    slot_lists = face_lists[0]
    slot_counts = face_counts[0]
    corner_index = corner_map[0]
    face_total, slot_total = slot_lists.shape
    width = operator_block.shape[0]
    loads = local_loads.shape[1]
    coarse_total = coarse_inverse.shape[1]
    row_length = lax.axis_size("sub") // 4
    usable = (
        lax.broadcasted_iota(jnp.int32, (face_total, slot_total), 1) < slot_counts[:, None]
    ).astype(jnp.float32)
    flat_slots = slot_lists.reshape(-1)
    shared = jnp.zeros((width,), jnp.float32).at[flat_slots].add(usable.reshape(-1))
    weight = 1.0 / (1.0 + shared)
    widened = coupling.astype(jnp.float32)

    def assemble(values):
        height = values.shape[0]
        outgoing = values[:, flat_slots].reshape(height, face_total, slot_total)
        left_piece = shifted(outgoing[:, 1], "sub", 1)
        right_piece = shifted(outgoing[:, 0], "sub", -1)
        upper_piece = shifted(outgoing[:, 3], "sub", row_length)
        lower_piece = shifted(outgoing[:, 2], "sub", -row_length)
        received_values = (
            jnp.stack([left_piece, right_piece, upper_piece, lower_piece], axis=1) * usable[None]
        )
        return values.at[:, flat_slots].add(received_values.reshape(height, -1))

    def gram(leading_part, trailing_part):
        return lax.psum(
            jnp.einsum("lm,km->lk", leading_part * weight, trailing_part, precision=HIGH),
            ("coarse", "sub"),
        )

    every_corner = lax.all_gather(corner_index, ("coarse", "sub"), axis=0, tiled=True)
    diagonal = jnp.diagonal(operator_block).astype(jnp.float32)[None]
    combined = assemble(jnp.concatenate([local_loads[0], diagonal], axis=0))
    residual = combined[:loads]
    diagonal_sum = combined[loads:]
    precond = residual / diagonal_sum
    direction = precond
    precond_gram = gram(precond, residual)
    solution = jnp.zeros_like(residual)
    for iteration in range(ITERS):
        rounded = direction.astype(jnp.bfloat16)
        product = jnp.dot(rounded, operator_block, preferred_element_type=jnp.float32)
        corner_terms = jnp.dot(rounded, coupling.T, preferred_element_type=jnp.float32)
        everything = lax.all_gather(corner_terms, ("coarse", "sub"), axis=1, tiled=True)
        assembled = (
            jnp.zeros((loads, coarse_total), jnp.float32).at[:, every_corner].add(everything)
        )
        solved_rows = jnp.einsum("ln,kn->lk", assembled, coarse_inverse, precision=HIGH)
        solved = lax.all_gather(solved_rows, "coarse", axis=1, tiled=True)
        picked = solved[:, corner_index]
        image = product + jnp.dot(picked, widened, precision=HIGH)
        curvature = lax.psum(split_product(rounded, image), ("coarse", "sub"))
        image, curvature = (image, curvature)
        image = assemble(image)
        step_size = spd_solve(curvature, precond_gram)
        solution = solution + jnp.einsum("lk,lm->km", step_size, direction, precision=HIGH)
        residual = residual - jnp.einsum("lk,lm->km", step_size, image, precision=HIGH)
        if iteration + 1 < ITERS:
            precond = residual / diagonal_sum
            fresh = gram(precond, residual)
            blend = spd_solve(precond_gram, fresh)
            direction = precond + jnp.einsum("lk,lm->km", blend, direction, precision=HIGH)
            precond_gram = fresh
    return (solution[None], residual[None])


def solution(mesh):
    return jax.shard_map(
        local,
        mesh=mesh,
        in_specs=(
            P(("coarse", "sub"), None, None),
            P(("coarse", "sub"), None, None),
            P("coarse", None),
            P(("coarse", "sub"), None, None),
            P(("coarse", "sub"), None, None),
            P(("coarse", "sub"), None),
            P(("coarse", "sub"), None),
        ),
        out_specs=(P(("coarse", "sub"), None, None), P(("coarse", "sub"), None, None)),
        check_vma=False,
    )
```

profile of v0, /device:TPU:1, one launch (start us, length us, event | category | flops | bytes accessed | tf_op | source)
XLA Modules:
  0.0 1907.2 jit_solution(18435837209483688315)
XLA Ops:
  8.1 32.0 %gather_fusion = bf16[2048]{0:T(1024)(128)(2,1)S(1)} fusion(bf16[2048,2048]{1,0:T(8,128)(2,1)} %bitcast.241, s32[2048]{0:T(1024)S(1)} %bitcast.242), kind=kCustom, calls=%fused_computation | custom fusion | bytes 24576 | tf_op jit(solution)/shard_map/jit(diagonal)/cond/branch_0_fun/gather | solution.py:74
  44.4 4.7 gather_fusion.1
  49.1 2.5 slice_bitcast_fusion.3
  51.6 5.1 collective-permute-start
  58.1 4.7 collective-permute-start.2
  64.3 4.3 collective-permute-done.3
  68.6 8.6 collective-permute-done.2
  80.1 10.1 scatter_custom_fusion
  91.6 2.6 copy.69
  97.3 8.7 scatter_custom_fusion.2
  106.1 78.4 %all-reduce = s32[6144]{0:T(1024)S(1)} all-reduce(s32[6144]{0:T(1024)S(1)} %bitcast_dynamic-update-slice_fusion), channel_id=2, replica_groups=mesh['coarse'=8,'sub'=32] {'coarse','sub'}, use_global_device_ids=true, to_apply=%add | all-reduce | flops 6144 | bytes 49152 | tf_op jit(solution)/shard_map/all_gather | solution.py:73
  184.5 3.7 fusion.14
  188.2 5.7 fusion.87
  193.9 9.6 all-gather.5.cloned.1.call-done
  203.5 30.7 %scatter_custom_fusion.1 = f32[128,1536]{0,1:T(8,128)S(1)} fusion(s32[6144]{0:T(1024)S(1)} %compare_select_fusion, f32[128,6144]{0,1:T(8,128)} %all-gather.5.cloned.1.call-done, f32[]{:T(128)} %constant.48.clone.1), kind=kCustom, calls=%fused_computation.20 | custom fusion | flops 786432 | bytes 3932164 | tf_op jit(solution)/shard_map/scatter-add | solution.py:88
  235.4 14.1 all_gather.23
  250.0 1.8 convolution_add_fusion.2
  253.9 2.0 convolution_add_fusion.11
  255.9 2.6 gather_fusion.3
  259.4 3.0 collective-permute-start.4
  263.7 4.0 collective-permute-start.6
  269.2 228.9 %all-reduce.16.cloned.1.call-done = (f32[128,128]{0,1:T(8,128)}, f32[128,128]{0,1:T(8,128)}) async-done(((f32[128,128]{0,1:T(8,128)}, f32[128,128]{0,1:T(8,128)}), (f32[128,128]{0,1:T(8,128)}, f32[128,128]{0,1:T(8,128)})) %all-reduce.16.cloned.1.call-update) | async-done | bytes 131088 | tf_op jit(solution)/shard_map/psum | solution.py:68
  500.9 11.7 cholesky.100
  513.3 11.7 cholesky.89
  526.3 9.8 custom-call.19
  539.7 9.8 scatter_custom_fusion.3
  554.0 9.8 custom-call.21
  563.8 225.2 %all-reduce.8.cloned.1.call-done = f32[128,128]{0,1:T(8,128)} async-done(((f32[128,128]{0,1:T(8,128)}), f32[128,128]{0,1:T(8,128)}) %all-reduce.8.cloned.1.call-update) | async-done | bytes 65552 | tf_op jit(solution)/shard_map/psum | solution.py:68
  790.4 3.3 fusion.92
  795.2 11.7 cholesky.122
  807.6 5.6 fusion.85
  813.2 83.3 %all-gather.7.cloned.1.call-done = f32[128,6144]{0,1:T(8,128)} async-done(((f32[128,24]{0,1:T(8,128)}), f32[128,6144]{0,1:T(8,128)}) %all-gather.7.cloned.1.call-update) | async-done | bytes 3145744 | tf_op jit(solution)/shard_map/all_gather | solution.py:86
  896.6 30.7 %scatter_custom_fusion.4 = f32[128,1536]{0,1:T(8,128)S(1)} fusion(s32[6144]{0:T(1024)} %copy-done.22, f32[128,6144]{0,1:T(8,128)} %all-gather.7.cloned.1.call-done, f32[]{:T(128)} %constant.48.clone.1), kind=kCustom, calls=%fused_computation.18 | custom fusion | flops 786432 | bytes 3932672 | tf_op jit(solution)/shard_map/scatter-add | solution.py:88
  928.4 13.8 all_gather.25
  942.8 1.8 convolution_add_fusion.1
  947.3 2.0 convolution_add_fusion.9
  949.3 2.6 gather_fusion.5
  952.8 2.9 collective-permute-start.8
  957.0 4.0 collective-permute-start.10
  962.5 223.3 %all-reduce.10.cloned.1.call-done = f32[128,128]{0,1:T(8,128)} async-done(((f32[128,128]{0,1:T(8,128)}), f32[128,128]{0,1:T(8,128)}) %all-reduce.10.cloned.1.call-update) | async-done | bytes 65552 | tf_op jit(solution)/shard_map/psum | solution.py:94
  1187.6 11.7 cholesky.111
  1200.7 9.8 custom-call.23
  1213.2 9.6 scatter_custom_fusion.5
  1224.9 1.7 fusion.10
  1227.6 9.8 custom-call.25
  1237.4 223.4 %all-reduce.12.cloned.1.call-done = f32[128,128]{1,0:T(8,128)} async-done(((f32[128,128]{1,0:T(8,128)}), f32[128,128]{1,0:T(8,128)}) %all-reduce.12.cloned.1.call-update) | async-done | bytes 65552 | tf_op jit(solution)/shard_map/psum | solution.py:68
  1462.1 3.7 fusion.93
  1468.0 2.0 convolution_add_fusion.5
  1470.0 5.6 fusion.83
  1475.6 93.0 %all-gather.9.cloned.1.call-done = f32[128,6144]{0,1:T(8,128)} async-done(((f32[128,24]{0,1:T(8,128)}), f32[128,6144]{0,1:T(8,128)}) %all-gather.9.cloned.1.call-update) | async-done | bytes 3145744 | tf_op jit(solution)/shard_map/all_gather | solution.py:86
  1568.7 30.7 %scatter_custom_fusion.6 = f32[128,1536]{0,1:T(8,128)S(1)} fusion(s32[6144]{0:T(1024)} %copy-done.22, f32[128,6144]{0,1:T(8,128)} %all-gather.9.cloned.1.call-done, f32[]{:T(128)} %constant.48.clone.1), kind=kCustom, calls=%fused_computation.16 | custom fusion | flops 786432 | bytes 3932672 | tf_op jit(solution)/shard_map/scatter-add | solution.py:88
  1600.5 14.1 all_gather.27
  1615.1 1.8 convolution_add_fusion
  1619.0 2.0 convolution_add_fusion.7
  1621.0 3.7 gather_fusion.7
  1624.7 2.2 slice_bitcast_fusion.7
  1626.9 3.6 collective-permute-start.12
  1631.8 4.7 collective-permute-start.14
  1637.7 219.7 %all-reduce.14.cloned.1.call-done = f32[128,128]{0,1:T(8,128)} async-done(((f32[128,128]{0,1:T(8,128)}), f32[128,128]{0,1:T(8,128)}) %all-reduce.14.cloned.1.call-update) | async-done | bytes 65552 | tf_op jit(solution)/shard_map/psum | solution.py:94
  1859.2 11.7 cholesky.133
  1872.3 9.8 custom-call.27
  1882.6 3.2 fusion.7
  1888.3 9.6 scatter_custom_fusion.7
  1897.9 2.0 fusion.6
  (182 shorter events, 71.4 us)
Async XLA Ops:
  7.2 227.1 %copy-start = (f32[192,1536]{1,0:T(8,128)S(1)}, f32[192,1536]{1,0:T(8,128)}, u32[]{:S(2)}) copy-start(f32[192,1536]{1,0:T(8,128)} %param.14) | copy-start | bytes 3538948
  7.2 196.3 %all-gather.5.cloned.1.call-start = ((), (), s32[]{:S(2)}) async-start(), calls=%async_computation | async-start | bytes 3158016 | tf_op jit(solution)/shard_map/all_gather | solution.py:86
  8.1 33.4 %copy-start.16 = (f32[1,128,2048]{2,1,0:T(8,128)S(1)}, f32[1,128,2048]{2,1,0:T(8,128)}, u32[]{:S(2)}) copy-start(f32[1,128,2048]{2,1,0:T(8,128)} %param.15) | copy-start | bytes 3145732
  49.1 15.0 copy-start.25
  51.6 12.7 collective-permute-start
  56.8 11.9 collective-permute-start.3
  58.1 19.2 %collective-permute-start.2 = (f32[129,384]{0,1:T(8,128)}, f32[129,384]{0,1:T(8,128)}, u32[]{:S(2)}, u32[]{:S(2)}) collective-permute-start(f32[129,384]{0,1:T(8,128)} %get-tuple-element.9), channel_id=1, source_target_pairs={{0,8},{1,9},{2,10},{3,11},{4,12},{5,13},{6,14},{7,15},{8,16},{9,17... | collective-permute-start | bytes 594440 | tf_op jit(solution)/shard_map/ppermute | solution.py:15
  62.8 14.4 collective-permute-start.1
  91.6 4.7 copy-start.13
  91.6 14.3 copy-start.26
  95.5 0.8 copy-start.1
  97.2 400.9 %all-reduce.16.cloned.1.call-start = ((), (), s32[]{:S(2)}) async-start(), calls=%async_computation.7 | async-start | bytes 262144 | tf_op jit(solution)/shard_map/psum | solution.py:68
  184.5 366.1 %copy-start.23 = (f32[2048]{0:T(1024)}, f32[2048]{0:T(1024)S(1)}, u32[]{:S(2)}) copy-start(f32[2048]{0:T(1024)S(1)} %broadcast_divide_fusion.5) | copy-start | bytes 24580
  184.5 19.0 copy-start.22
  184.5 3.7 copy-start.2
  235.3 16.5 copy-start.3
  258.5 530.5 %all-reduce.8.cloned.1.call-start = ((), (), s32[]{:S(2)}) async-start(), calls=%async_computation.1 | async-start | bytes 131072 | tf_op jit(solution)/shard_map/psum | solution.py:68
  259.4 278.1 %collective-permute-start.4 = (f32[128,384]{0,1:T(8,128)}, f32[128,384]{0,1:T(8,128)S(1)}, u32[]{:S(2)}, u32[]{:S(2)}) collective-permute-start(f32[128,384]{0,1:T(8,128)} %get-tuple-element.19), channel_id=1, source_target_pairs={{0,1},{1,2},{2,3},{3,4},{4,5},{5,6},{6,7},{7,8},{8,9},{9,10},{10,1... | collective-permute-start | bytes 589832 | tf_op jit(solution)/shard_map/ppermute | solution.py:15
  262.4 275.1 %collective-permute-start.7 = (f32[128,384]{0,1:T(8,128)}, f32[128,384]{0,1:T(8,128)S(1)}, u32[]{:S(2)}, u32[]{:S(2)}) collective-permute-start(f32[128,384]{0,1:T(8,128)} %get-tuple-element.20), channel_id=1, source_target_pairs={{8,0},{9,1},{10,2},{11,3},{12,4},{13,5},{14,6},{15,7},{16,8},{17,9... | collective-permute-start | bytes 589832 | tf_op jit(solution)/shard_map/ppermute | solution.py:15
  263.7 273.8 %collective-permute-start.6 = (f32[128,384]{0,1:T(8,128)}, f32[128,384]{0,1:T(8,128)S(1)}, u32[]{:S(2)}, u32[]{:S(2)}) collective-permute-start(f32[128,384]{0,1:T(8,128)} %get-tuple-element.21), channel_id=1, source_target_pairs={{0,8},{1,9},{2,10},{3,11},{4,12},{5,13},{6,14},{7,15},{8,16},{9,17... | collective-permute-start | bytes 589832 | tf_op jit(solution)/shard_map/ppermute | solution.py:15
  267.7 269.8 %collective-permute-start.5 = (f32[128,384]{0,1:T(8,128)S(1)}, f32[128,384]{0,1:T(8,128)}, u32[]{:S(2)}, u32[]{:S(2)}) collective-permute-start(f32[128,384]{0,1:T(8,128)S(1)} %get-tuple-element.22), channel_id=1, source_target_pairs={{1,0},{2,1},{3,2},{4,3},{5,4},{6,5},{7,6},{8,7},{9,8},{10,9},{11,1... | collective-permute-start | bytes 589832 | tf_op jit(solution)/shard_map/ppermute | solution.py:15
  512.6 13.7 copy-start.20
  538.5 11.0 copy-start.6
  550.6 1.0 copy-start.10
  551.5 1.8 copy-start.21
  553.3 343.3 %all-gather.7.cloned.1.call-start = ((), (), s32[]{:S(2)}) async-start(), calls=%async_computation.2 | async-start | bytes 3158016 | tf_op jit(solution)/shard_map/all_gather | solution.py:86
  790.4 4.7 copy-start.15
  793.7 150.9 %copy-start.5 = (bf16[128,2048]{1,0:T(8,128)(2,1)}, bf16[128,2048]{1,0:T(8,128)(2,1)S(1)}, u32[]{:S(2)}) copy-start(bf16[128,2048]{1,0:T(8,128)(2,1)S(1)} %get-tuple-element.25) | copy-start | bytes 1572868
  794.6 391.2 %all-reduce.10.cloned.1.call-start = ((), (), s32[]{:S(2)}) async-start(), calls=%async_computation.3 | async-start | bytes 131072 | tf_op jit(solution)/shard_map/psum | solution.py:94
  806.9 6.4 copy-start.18
  949.3 511.5 %all-reduce.12.cloned.1.call-start = ((), (), s32[]{:S(2)}) async-start(), calls=%async_computation.4 | async-start | bytes 131072 | tf_op jit(solution)/shard_map/psum | solution.py:68
  952.8 258.3 %collective-permute-start.8 = (f32[128,384]{0,1:T(8,128)}, f32[128,384]{0,1:T(8,128)S(1)}, u32[]{:S(2)}, u32[]{:S(2)}) collective-permute-start(f32[128,384]{0,1:T(8,128)} %get-tuple-element.15), channel_id=1, source_target_pairs={{0,1},{1,2},{2,3},{3,4},{4,5},{5,6},{6,7},{7,8},{8,9},{9,10},{10,1... | collective-permute-start | bytes 589832 | tf_op jit(solution)/shard_map/ppermute | solution.py:15
  955.7 255.3 %collective-permute-start.11 = (f32[128,384]{0,1:T(8,128)}, f32[128,384]{0,1:T(8,128)S(1)}, u32[]{:S(2)}, u32[]{:S(2)}) collective-permute-start(f32[128,384]{0,1:T(8,128)} %get-tuple-element.16), channel_id=1, source_target_pairs={{8,0},{9,1},{10,2},{11,3},{12,4},{13,5},{14,6},{15,7},{16,8},{17,9... | collective-permute-start | bytes 589832 | tf_op jit(solution)/shard_map/ppermute | solution.py:15
  957.0 254.1 %collective-permute-start.10 = (f32[128,384]{0,1:T(8,128)}, f32[128,384]{0,1:T(8,128)S(1)}, u32[]{:S(2)}, u32[]{:S(2)}) collective-permute-start(f32[128,384]{0,1:T(8,128)} %get-tuple-element.17), channel_id=1, source_target_pairs={{0,8},{1,9},{2,10},{3,11},{4,12},{5,13},{6,14},{7,15},{8,16},{9,17... | collective-permute-start | bytes 589832 | tf_op jit(solution)/shard_map/ppermute | solution.py:15
  961.0 250.1 %collective-permute-start.9 = (f32[128,384]{0,1:T(8,128)S(1)}, f32[128,384]{0,1:T(8,128)}, u32[]{:S(2)}, u32[]{:S(2)}) collective-permute-start(f32[128,384]{0,1:T(8,128)S(1)} %get-tuple-element.18), channel_id=1, source_target_pairs={{1,0},{2,1},{3,2},{4,3},{5,4},{6,5},{7,6},{8,7},{9,8},{10,9},{11,1... | collective-permute-start | bytes 589832 | tf_op jit(solution)/shard_map/ppermute | solution.py:15
  1212.0 10.7 copy-start.11
  1213.2 11.7 copy-start.24
  1223.9 1.0 copy-start.8
  1224.8 2.0 copy-start.19
  1226.6 342.1 %all-gather.9.cloned.1.call-start = ((), (), s32[]{:S(2)}) async-start(), calls=%async_computation.5 | async-start | bytes 3158016 | tf_op jit(solution)/shard_map/all_gather | solution.py:86
  1462.1 4.7 copy-start.7
  1465.8 151.1 %copy-start.4 = (bf16[128,2048]{1,0:T(8,128)(2,1)}, bf16[128,2048]{1,0:T(8,128)(2,1)S(1)}, u32[]{:S(2)}) copy-start(bf16[128,2048]{1,0:T(8,128)(2,1)S(1)} %get-tuple-element.27) | copy-start | bytes 1572868
  1466.7 390.7 %all-reduce.14.cloned.1.call-start = ((), (), s32[]{:S(2)}) async-start(), calls=%async_computation.6 | async-start | bytes 131072 | tf_op jit(solution)/shard_map/psum | solution.py:94
  1466.8 1.2 copy-start.14
  1624.7 257.4 %copy-start.17 = (f32[128,128]{1,0:T(8,128)S(1)}, f32[128,128]{1,0:T(8,128)}, u32[]{:S(2)}) copy-start(f32[128,128]{1,0:T(8,128)} %all-reduce.12.cloned.1.call-done) | copy-start | bytes 196612
  1624.7 257.9 %copy-start.12 = (f32[128,2048]{1,0:T(8,128)S(1)}, f32[128,2048]{1,0:T(8,128)}, u32[]{:S(2)}) copy-start(f32[128,2048]{1,0:T(8,128)} %convolution_add_fusion.5) | copy-start | bytes 3145732
  1626.9 259.0 %collective-permute-start.12 = (f32[128,384]{0,1:T(8,128)}, f32[128,384]{0,1:T(8,128)}, u32[]{:S(2)}, u32[]{:S(2)}) collective-permute-start(f32[128,384]{0,1:T(8,128)} %get-tuple-element.11), channel_id=1, source_target_pairs={{0,1},{1,2},{2,3},{3,4},{4,5},{5,6},{6,7},{7,8},{8,9},{9,10},{10,1... | collective-permute-start | bytes 589832 | tf_op jit(solution)/shard_map/ppermute | solution.py:15
  1630.5 255.4 %collective-permute-start.15 = (f32[128,384]{0,1:T(8,128)}, f32[128,384]{0,1:T(8,128)}, u32[]{:S(2)}, u32[]{:S(2)}) collective-permute-start(f32[128,384]{0,1:T(8,128)} %get-tuple-element.12), channel_id=1, source_target_pairs={{8,0},{9,1},{10,2},{11,3},{12,4},{13,5},{14,6},{15,7},{16,8},{17,9... | collective-permute-start | bytes 589832 | tf_op jit(solution)/shard_map/ppermute | solution.py:15
  1631.8 254.1 %collective-permute-start.14 = (f32[128,384]{0,1:T(8,128)}, f32[128,384]{0,1:T(8,128)}, u32[]{:S(2)}, u32[]{:S(2)}) collective-permute-start(f32[128,384]{0,1:T(8,128)} %get-tuple-element.13), channel_id=1, source_target_pairs={{0,8},{1,9},{2,10},{3,11},{4,12},{5,13},{6,14},{7,15},{8,16},{9,17... | collective-permute-start | bytes 589832 | tf_op jit(solution)/shard_map/ppermute | solution.py:15
  1636.4 249.4 %collective-permute-start.13 = (f32[128,384]{0,1:T(8,128)}, f32[128,384]{0,1:T(8,128)}, u32[]{:S(2)}, u32[]{:S(2)}) collective-permute-start(f32[128,384]{0,1:T(8,128)} %get-tuple-element.14), channel_id=1, source_target_pairs={{1,0},{2,1},{3,2},{4,3},{5,4},{6,5},{7,6},{8,7},{9,8},{10,9},{11,1... | collective-permute-start | bytes 589832 | tf_op jit(solution)/shard_map/ppermute | solution.py:15
  1887.2 10.7 copy-start.9
Sparse Core Ops, SparseCore 0:
  97.3 106.1 all-gather.4
  258.6 239.4 all-reduce.15
  553.4 235.5 all-reduce.7
  794.7 101.8 all-gather.6
  949.4 236.3 all-reduce.9
  1226.7 234.0 all-reduce.11
  1466.8 101.8 all-gather.8
  1621.1 236.2 all-reduce.13
where the time goes:
time: 1920 us; the launch traced here: 1910 us
  waiting for transfers between devices  1320 us (69%)
  other arithmetic  270 us (14%)
  blocking collectives  120 us (6%)
  matrix products  69.5 us (4%)
  local copies, waits for them, and re-layouts  69.1 us (4%)
  starting transfers between devices  43.6 us (2%)
    psum x3, waiting for transfers between devices, gram(): lax.psum(jnp.einsum('lm,km->lk', leading_part * weight, trailing_part, pr...  678 us
    psum x2, waiting for transfers between devices, local(): curvature = lax.psum(split_product(rounded, image), ('coarse', 'sub'))  443 us
    all_gather x3, waiting for transfers between devices, local(): lax.all_gather(corner_terms, ('coarse', 'sub'), axis=1, tiled=True)  186 us
    scatter-add x3, other arithmetic, local(): jnp.zeros((loads, coarse_total), jnp.float32).at[:, every_corner]  92.1 us
    all_gather x1, blocking collectives, local(): lax.all_gather(corner_index, ('coarse', 'sub'), axis=0, tiled=True)  78.4 us
    another operation x15, other arithmetic, spd_solve(): factor = jnp.linalg.cholesky(matrix)  62.1 us
    another operation x10, other arithmetic, spd_solve(): lax.linalg.triangular_solve(factor, middle, left_side=True, lower=True, t...  52.3 us
    ppermute x16, starting transfers between devices, shifted(): lax.ppermute(value, axis, [(source, source + steps) for source in range(f...  42.7 us
  transfers between devices with their start and end apart: 24, of which 10 were waited for; matrix products, arithmetic and copies ran while one was open for 9% of the time, Pallas kernels for 0%

commit v1 on v0

v1 whole, which is shorter than its diff:
```python
import jax
import jax.numpy as jnp
from jax import lax
from jax.experimental import pallas as pl
from jax.experimental.pallas import tpu as pltpu
from jax.sharding import PartitionSpec as P

ITERS = 3
HIGH = lax.Precision.HIGHEST
MESH = pl.DeviceIdType.MESH
F32, BF16 = jnp.float32, jnp.bfloat16
VMEM = pl.BlockSpec(memory_space=pltpu.VMEM)


def parts_of(values, count):
    parts = []
    for _ in range(count):
        part = lax.reduce_precision(values, 8, 7)
        parts.append(part.astype(BF16))
        values = values - part
    return parts


def greet(groups):
    barrier = pltpu.get_barrier_semaphore()
    for axis, count in groups:
        me = lax.axis_index(axis)

        def one(step, carry, axis=axis, count=count, me=me):
            pl.semaphore_signal(
                barrier,
                inc=1,
                device_id={axis: lax.rem(me + step, count)},
                device_id_type=MESH,
            )
            return carry

        lax.fori_loop(1, count, one, 0)
    pl.semaphore_wait(barrier, sum(count - 1 for _, count in groups))


def send_all(axis, count, pick, landing, sems):
    me = lax.axis_index(axis)

    def one(step, carry):
        peer = lax.rem(me + step, count)
        pltpu.make_async_remote_copy(
            src_ref=pick(peer),
            dst_ref=landing.at[me],
            send_sem=sems.at[0],
            recv_sem=sems.at[1],
            device_id={axis: peer},
            device_id_type=MESH,
        ).start()
        return carry

    lax.fori_loop(1, count, one, 0)


def wait_all(count, landing, sems):
    whole = landing.at[pl.ds(0, count - 1)]
    pltpu.make_async_copy(whole, whole, sems.at[1]).wait()
    pltpu.make_async_copy(whole, whole, sems.at[0]).wait()


def sum_slots(count, landing):
    total = landing[0]
    for slot in range(1, count):
        total = total + landing[slot]
    return total


def stacked_dot(rows, matrix):
    first = rows.astype(BF16).astype(F32)
    rest = rows - first
    second = rest.astype(BF16).astype(F32)
    third = rest - second
    stack = jnp.concatenate([first, second, third, jnp.zeros_like(rows)], axis=0).astype(BF16)
    full = jnp.dot(stack, matrix, preferred_element_type=F32)
    return full[0:4] + full[4:8] + full[8:12]


def all_sum_kernel(n_sub, n_coarse, x_ref, out_ref, first, middle, second, sems):
    me, group = lax.axis_index("sub"), lax.axis_index("coarse")
    greet((("sub", n_sub), ("coarse", n_coarse)))
    first[me] = x_ref[me]
    send_all("sub", n_sub, lambda peer: x_ref.at[peer], first, sems.at[0])
    wait_all(n_sub, first, sems.at[0])
    partial = sum_slots(n_sub, first)
    middle[...] = partial
    second[group] = partial
    send_all("coarse", n_coarse, lambda peer: middle, second, sems.at[1])
    wait_all(n_coarse, second, sems.at[1])
    total = sum_slots(n_coarse, second)
    middle[...] = total
    out_ref[me] = total
    send_all("sub", n_sub, lambda peer: middle, out_ref, sems.at[2])
    wait_all(n_sub, out_ref, sems.at[2])


def all_sum(x, sizes, collective_id):
    n_sub, n_coarse = sizes
    height, width = x.shape
    rows = height // n_sub
    slots = lambda count: pltpu.VMEM((count, rows, width), F32)
    out = pl.pallas_call(
        lambda *refs: all_sum_kernel(n_sub, n_coarse, *refs),
        out_shape=jax.ShapeDtypeStruct((n_sub, rows, width), F32),
        in_specs=[VMEM],
        out_specs=VMEM,
        scratch_shapes=[
            slots(n_sub),
            pltpu.VMEM((rows, width), F32),
            slots(n_coarse),
            pltpu.SemaphoreType.DMA((3, 2)),
        ],
        compiler_params=pltpu.CompilerParams(collective_id=collective_id, has_side_effects=True),
    )(x.reshape(n_sub, rows, width))
    return out.reshape(height, width)


def gather_kernel(n_sub, x_ref, out_ref, sems):
    me = lax.axis_index("sub")
    greet((("sub", n_sub),))
    out_ref[me] = x_ref[...]
    send_all("sub", n_sub, lambda peer: x_ref, out_ref, sems)
    wait_all(n_sub, out_ref, sems)


def gather_group(x, n_sub, collective_id):
    return pl.pallas_call(
        lambda *refs: gather_kernel(n_sub, *refs),
        out_shape=jax.ShapeDtypeStruct((n_sub,) + x.shape, x.dtype),
        in_specs=[VMEM],
        out_specs=VMEM,
        scratch_shapes=[pltpu.SemaphoreType.DMA((2,))],
        compiler_params=pltpu.CompilerParams(collective_id=collective_id, has_side_effects=True),
    )(x)


def corner_kernel(
    n_sub, n_coarse, terms_ref, spread_ref, pick_ref, inverse_ref, out_ref,
    first, partial_rows, second, solved_rows, third, picks, sems,
):
    me, group = lax.axis_index("sub"), lax.axis_index("coarse")
    greet((("sub", n_sub), ("coarse", n_coarse)))
    first[me] = terms_ref[me]
    send_all("sub", n_sub, lambda peer: terms_ref.at[peer], first, sems.at[0])
    wait_all(n_sub, first, sems.at[0])
    tiles = [
        first[4 * t] + first[4 * t + 1] + first[4 * t + 2] + first[4 * t + 3]
        for t in range(n_sub // 4)
    ]
    partial = stacked_dot(jnp.concatenate(tiles, axis=1), spread_ref[...])
    partial_rows[...] = partial
    second[group] = partial
    send_all("coarse", n_coarse, lambda peer: partial_rows, second, sems.at[1])
    wait_all(n_coarse, second, sems.at[1])
    assembled = sum_slots(n_coarse, second)
    wide = stacked_dot(assembled, inverse_ref[...])
    solved = wide[:, 0:256] + wide[:, 256:512] + wide[:, 512:768]
    solved_rows[...] = solved
    third[group] = solved
    send_all("coarse", n_coarse, lambda peer: solved_rows, third, sems.at[2])
    wait_all(n_coarse, third, sems.at[2])
    everything = jnp.concatenate([third[c] for c in range(n_coarse)], axis=1)
    picked = stacked_dot(everything, pick_ref[...])
    for t in range(n_sub // 4):
        picks[t] = picked[:, 128 * t : 128 * (t + 1)]
    out_ref[me] = picks[me // 4]
    send_all("sub", n_sub, lambda peer: picks.at[peer // 4], out_ref, sems.at[3])
    wait_all(n_sub, out_ref, sems.at[3])


def corner_solve(terms, spread, pick, inverse, sizes, collective_id):
    n_sub, n_coarse = sizes
    height, width = terms.shape
    rows = height // n_sub
    span = spread.shape[1]
    out = pl.pallas_call(
        lambda *refs: corner_kernel(n_sub, n_coarse, *refs),
        out_shape=jax.ShapeDtypeStruct((n_sub, rows, width), F32),
        in_specs=[VMEM] * 4,
        out_specs=VMEM,
        scratch_shapes=[
            pltpu.VMEM((n_sub, rows, width), F32),
            pltpu.VMEM((rows, span), F32),
            pltpu.VMEM((n_coarse, rows, span), F32),
            pltpu.VMEM((rows, 256), F32),
            pltpu.VMEM((n_coarse, rows, 256), F32),
            pltpu.VMEM((n_sub // 4, rows, width), F32),
            pltpu.SemaphoreType.DMA((4, 2)),
        ],
        compiler_params=pltpu.CompilerParams(
            collective_id=collective_id, has_side_effects=True, vmem_limit_bytes=40 << 20
        ),
    )(terms.reshape(n_sub, rows, width), spread, pick, inverse)
    return out.reshape(height, width)


def solve_kernel(matrix_ref, right_ref, out_ref, work):
    size = matrix_ref.shape[0]
    work[:, 0:size] = matrix_ref[...]
    work[:, size : 2 * size] = right_ref[...]
    row_at = lax.broadcasted_iota(jnp.int32, (size, 1), 0)

    def block(step, carry):
        left = work[:, 0:size]
        right = work[:, size : 2 * size]
        for inner in range(8):
            pivot_at = step * 8 + inner
            mark = row_at == pivot_at
            start = pl.multiple_of(step * 8, 8)
            column = left[:, inner : inner + 1]
            pivot_left = jnp.sum(jnp.where(mark, left, 0.0), axis=0, keepdims=True)
            pivot_right = jnp.sum(jnp.where(mark, right, 0.0), axis=0, keepdims=True)
            scale = 1.0 / pivot_left[:, inner : inner + 1]
            pivot_left = pivot_left * scale
            pivot_right = pivot_right * scale
            left = jnp.where(mark, pivot_left, left - column * pivot_left)
            right = jnp.where(mark, pivot_right, right - column * pivot_right)
        work[:, 0:size] = pltpu.roll(left, size - 8, 1)
        work[:, size : 2 * size] = right
        return carry

    lax.fori_loop(0, size // 8, block, 0)
    out_ref[...] = work[:, size : 2 * size]


def spd_solve(matrix, right):
    size = matrix.shape[0]
    return pl.pallas_call(
        solve_kernel,
        out_shape=jax.ShapeDtypeStruct(right.shape, F32),
        in_specs=[VMEM, VMEM],
        out_specs=VMEM,
        scratch_shapes=[pltpu.VMEM((size, 2 * size), F32)],
    )(matrix, right)


def shifted(value, axis, steps):
    count = lax.axis_size(axis)
    first, last = (max(0, -steps), min(count, count - steps))
    return lax.ppermute(value, axis, [(source, source + steps) for source in range(first, last)])


def local(
    local_operators, couplings, coarse_inverse, local_loads, face_lists, face_counts, corner_map
):
    operator_block = local_operators[0]
    coupling = couplings[0]
    slot_lists = face_lists[0]
    face_total, slot_total = slot_lists.shape
    width = operator_block.shape[0]
    loads = local_loads.shape[1]
    corners = coupling.shape[0]
    n_sub, n_coarse = lax.axis_size("sub"), lax.axis_size("coarse")
    sizes = (n_sub, n_coarse)
    row_length = n_sub // 4
    me = lax.axis_index("sub")

    usable = lax.broadcasted_iota(jnp.int32, (face_total, slot_total), 1) < face_counts[0][:, None]
    marked = jnp.where(usable, slot_lists, -1).reshape(-1)
    hot = (
        marked[:, None] == lax.broadcasted_iota(jnp.int32, (face_total * slot_total, width), 1)
    ).astype(BF16)
    weight = 1.0 / (1.0 + jnp.sum(hot.astype(F32), axis=0))[None]

    rows = coarse_inverse.shape[0]
    maps = jnp.full((1, 128), -1, jnp.int32).at[:, :corners].set(corner_map)
    every = gather_group(maps, n_sub, 0)[:, 0, :32].reshape(-1)
    place = jnp.where(every < 0, -1, every // rows * 256 + every % rows)
    span = n_coarse * 256
    spread = (place[:, None] == lax.broadcasted_iota(jnp.int32, (n_sub * 32, span), 1)).astype(BF16)
    pick = (place[None, :] == lax.broadcasted_iota(jnp.int32, (span, n_sub * 32), 0)).astype(BF16)
    turned = coarse_inverse.T.reshape(n_coarse, rows, rows)
    turned = jnp.pad(turned, ((0, 0), (0, 256 - rows), (0, 256 - rows))).reshape(span, 256)
    inverse = jnp.concatenate(parts_of(turned, 3), axis=1)
    coupling_at = lax.dynamic_update_slice(
        jnp.zeros((128, width), BF16), coupling, (lax.rem(me, 4) * 32, 0)
    )

    def assemble(values, count):
        height = values.shape[0]
        pieces = jnp.concatenate(parts_of(values, count), axis=0)
        outgoing = lax.dot_general(
            pieces, hot, (((1,), (1,)), ((), ())), preferred_element_type=F32
        )
        outgoing = outgoing.reshape(count, height, -1).sum(0)
        outgoing = outgoing.reshape(height, face_total, slot_total)
        received = jnp.concatenate(
            [
                shifted(outgoing[:, 1], "sub", 1),
                shifted(outgoing[:, 0], "sub", -1),
                shifted(outgoing[:, 3], "sub", row_length),
                shifted(outgoing[:, 2], "sub", -row_length),
            ],
            axis=1,
        )
        pieces = jnp.concatenate(parts_of(received, count), axis=0)
        added = jnp.dot(pieces, hot, preferred_element_type=F32)
        return values + added.reshape(count, height, -1).sum(0)

    def cross(leading, trailing):
        return jnp.einsum("lm,km->lk", leading, trailing, precision=HIGH)

    block = 128
    diagonal = jnp.concatenate(
        [
            jnp.sum(
                jnp.where(
                    jnp.eye(block, dtype=bool),
                    operator_block[at : at + block, at : at + block].astype(F32),
                    0.0,
                ),
                axis=0,
            )
            for at in range(0, width, block)
        ]
    )[None]
    combined = assemble(jnp.concatenate([local_loads[0], diagonal], axis=0), 3)
    residual = combined[:loads]
    scaled = weight / combined[loads:]
    inverse_diagonal = 1.0 / combined[loads:]
    precond = residual * inverse_diagonal
    direction = precond
    precond_gram = all_sum(cross(residual * scaled, residual), sizes, 1)
    solution = jnp.zeros_like(residual)
    for iteration in range(ITERS):
        last = iteration + 1 == ITERS
        rounded = direction.astype(BF16)
        terms = lax.dot_general(
            rounded, coupling_at, (((1,), (1,)), ((), ())), preferred_element_type=F32
        )
        picked = corner_solve(terms, spread, pick, inverse, sizes, 2)
        product = jnp.dot(rounded, operator_block, preferred_element_type=F32)
        image = product + jnp.dot(picked, coupling_at.astype(F32), precision=HIGH)
        curvature = cross(rounded.astype(F32), image)
        image = assemble(image, 2)
        if last:
            curvature = all_sum(curvature, sizes, 1)
        else:
            weighted = image * scaled
            sums = jnp.concatenate(
                [curvature, cross(weighted, residual), cross(weighted, image)], axis=1
            )
            sums = all_sum(sums, sizes, 3)
            curvature, mixed, square = sums[:, :loads], sums[:, loads : 2 * loads], sums[:, 2 * loads :]
        step_size = spd_solve(curvature, precond_gram)
        solution = solution + jnp.einsum("lk,lm->km", step_size, direction, precision=HIGH)
        residual = residual - jnp.einsum("lk,lm->km", step_size, image, precision=HIGH)
        if not last:
            turn = jnp.dot(step_size.T, mixed, precision=HIGH)
            fresh = (
                precond_gram
                - turn
                - turn.T
                + jnp.dot(step_size.T, jnp.dot(square, step_size, precision=HIGH), precision=HIGH)
            )
            blend = spd_solve(precond_gram, fresh)
            direction = residual * inverse_diagonal + jnp.einsum(
                "lk,lm->km", blend, direction, precision=HIGH
            )
            precond_gram = fresh
    return (solution[None], residual[None])


def solution(mesh):
    return jax.shard_map(
        local,
        mesh=mesh,
        in_specs=(
            P(("coarse", "sub"), None, None),
            P(("coarse", "sub"), None, None),
            P("coarse", None),
            P(("coarse", "sub"), None, None),
            P(("coarse", "sub"), None, None),
            P(("coarse", "sub"), None),
            P(("coarse", "sub"), None),
        ),
        out_specs=(P(("coarse", "sub"), None, None), P(("coarse", "sub"), None, None)),
        check_vma=False,
    )
```

time: 1920 us -> 520 us (0.27)
  waiting for transfers between devices: 1320 us -> 5.63 us
  Pallas kernels: 0 us -> 277 us
  other arithmetic: 270 us -> 42.6 us
  blocking collectives: 120 us -> 0 us
  local copies, waits for them, and re-layouts: 69.1 us -> 48.4 us
    psum x5 -> x0, waiting for transfers between devices: 1120 us -> none  [the longest x3 678 us: gram(): lax.psum(jnp.einsum('lm,km->lk', leading_part * weight, trailing_part, pr...]
    pallas_call x0 -> x13, Pallas kernels: none -> 277 us  [the longest x4 101 us: all_sum(): pl.pallas_call(lambda *refs: all_sum_kernel(n_sub, n_coarse, *refs), out_...]
    all_gather x3 -> x0, waiting for transfers between devices: 186 us -> none  [local(): lax.all_gather(corner_terms, ('coarse', 'sub'), axis=1, tiled=True)]
    scatter-add x8 -> x0, other arithmetic: 140 us -> none  [the longest x3 92.1 us: local(): jnp.zeros((loads, coarse_total), jnp.float32).at[:, every_corner]]
    all_gather x4 -> x0, blocking collectives: 120 us -> none  [the longest x1 78.4 us: local(): lax.all_gather(corner_index, ('coarse', 'sub'), axis=0, tiled=True)]
    another operation x29 -> x2, other arithmetic: 119 us -> 1.47 us  [the longest x15 62.1 us: spd_solve(): factor = jnp.linalg.cholesky(matrix)]
    gather x8 -> x0, local copies, waits for them, and re-layouts: 47.2 us -> none  [the longest x1 32 us: local(): diagonal = jnp.diagonal(operator_block).astype(jnp.float32)[None]]
    reduce_sum x0 -> x10, other arithmetic: none -> 20.3 us  [the longest x4 10.9 us: assemble(): return values + added.reshape(count, height, -1).sum(0)]
  transfers between devices with their start and end apart: 24 -> 16, of which waited for: 10 -> 3; matrix products, arithmetic and copies ran while one was open for 9% -> 7% of each run, Pallas kernels for 0% -> 14%
where the time goes in v1:
time: 520 us; the launch traced here: 512 us
  Pallas kernels  277 us (53%)
  matrix products  88.5 us (17%)
  local copies, waits for them, and re-layouts  48.4 us (9%)
  starting transfers between devices  47.9 us (9%)
  other arithmetic  42.6 us (8%)
  waiting for transfers between devices  5.63 us (1%)
    pallas_call x4, Pallas kernels, all_sum(): pl.pallas_call(lambda *refs: all_sum_kernel(n_sub, n_coarse, *refs), out_...  101 us
    pallas_call x3, Pallas kernels, corner_solve(): pl.pallas_call(lambda *refs: corner_kernel(n_sub, n_coarse, *refs), out_s...  81.9 us
    pallas_call x5, Pallas kernels, spd_solve(): pl.pallas_call(solve_kernel, out_shape=jax.ShapeDtypeStruct(right.shape,...  81.7 us
    ppermute x16, starting transfers between devices, shifted(): lax.ppermute(value, axis, [(source, source + steps) for source in range(f...  47.9 us
    unnamed x129, local copies, waits for them, and re-layouts  16.6 us
    dot_general x4, matrix products, assemble(): added = jnp.dot(pieces, hot, preferred_element_type=F32)  16.3 us
    dot_general x4, matrix products, assemble(): lax.dot_general(pieces, hot, (((1,), (1,)), ((), ())), preferred_element_...  16.2 us
    dot_general x3, matrix products, local(): product = jnp.dot(rounded, operator_block, preferred_element_type=F32)  14.9 us
  transfers between devices with their start and end apart: 16, of which 3 were waited for; matrix products, arithmetic and copies ran while one was open for 7% of the time, Pallas kernels for 14%

profile of v1, /device:TPU:1, one launch (start us, length us, event | category | flops | bytes accessed | tf_op | source)
XLA Modules:
  0.0 512.0 jit_solution(6008021117348056309)
XLA Ops:
  5.0 4.7 fusion.8
  9.7 1.9 reshape.212
  13.4 5.1 collective-permute-start
  20.5 7.7 %collective-permute-start.2 = (f32[129,384]{1,0:T(8,128)S(1)}, f32[129,384]{1,0:T(8,128)}, u32[]{:S(2)}, u32[]{:S(2)}) collective-permute-start(f32[129,384]{1,0:T(8,128)S(1)} %bitcast.167), channel_id=1, source_target_pairs={{0,8},{1,9},{2,10},{3,11},{4,12},{5,13},{6,14},{7,15},{8,16},{9,17... | collective-permute-start | bytes 594440 | tf_op jit(solution)/shard_map/ppermute | solution.py:244
  33.6 12.2 %shard_map.86 = s32[32,1,128]{2,1,0:T(1,128)} custom-call(s32[1,128]{1,0:T(1,128)} %scatter.4.refs_0_), custom_call_target="tpu_custom_call" | custom-call | tf_op jit(solution)/shard_map/pallas_call | solution.py:131
  47.8 2.7 fusion.9.refs_1_
  50.5 4.1 fusion.10.refs_2_
  55.2 2.4 reduce-precision_convert_fusion.1
  58.5 2.0 pad_maximum_fusion.refs_3_
  64.5 4.9 fusion.7
  69.4 4.0 reshape.214
  73.5 3.3 reduce_sum.242
  76.8 1.7 fusion.85
  79.6 4.8 fusion.116
  85.8 30.0 %shard_map.87 = f32[32,4,128]{2,1,0:T(4,128)S(1)} custom-call(f32[32,4,128]{2,1,0:T(4,128)S(1)} %bitcast.143, bf16[1024,2048]{1,0:T(8,128)(2,1)S(1)} %copy-done, bf16[2048,1024]{1,0:T(8,128)(2,1)S(1)} %copy-done.3, bf16[2048,768]{1,0:T(8,128)(2,1)S(1)} %pad_maximum_fusion.refs_3_), custom_call_target="tpu_custom_call" | custom-call | tf_op jit(solution)/shard_map/pallas_call | solution.py:180
  117.4 3.9 fusion.6
  121.3 2.5 reduce_sum.243
  123.8 2.3 reshape.220
  126.1 3.1 fusion.131
  129.9 2.9 collective-permute-start.4
  134.8 6.4 %collective-permute-start.6 = (f32[128,384]{1,0:T(8,128)S(1)}, f32[128,384]{1,0:T(8,128)}, u32[]{:S(2)}, u32[]{:S(2)}) collective-permute-start(f32[128,384]{1,0:T(8,128)S(1)} %bitcast.172), channel_id=1, source_target_pairs={{0,8},{1,9},{2,10},{3,11},{4,12},{5,13},{6,14},{7,15},{8,16},{9,17... | collective-permute-start | bytes 589832 | tf_op jit(solution)/shard_map/ppermute | solution.py:244
  145.5 22.8 %shard_map.89 = f32[32,4,128]{2,1,0:T(4,128)} custom-call(f32[32,4,128]{2,1,0:T(4,128)} %bitcast.164), custom_call_target="tpu_custom_call" | custom-call | tf_op jit(solution)/shard_map/pallas_call | solution.py:106
  172.3 3.8 fusion.5
  176.1 2.8 reduce_sum.244
  178.9 1.7 add.101
  183.7 26.8 %shard_map.88 = f32[32,4,384]{2,1,0:T(4,128)} custom-call(f32[32,4,384]{2,1,0:T(4,128)} %reshape.222.refs_0_), custom_call_target="tpu_custom_call" | custom-call | tf_op jit(solution)/shard_map/pallas_call | solution.py:106
  212.1 16.3 %shard_map.90 = f32[128,128]{1,0:T(8,128)} custom-call(f32[128,128]{1,0:T(8,128)} %slice.207.matrix_ref, f32[128,128]{1,0:T(8,128)} %bitcast.156), custom_call_target="tpu_custom_call" | custom-call | tf_op jit(solution)/shard_map/pallas_call | solution.py:232
  228.5 3.4 fusion.62
  231.9 1.7 fusion.97
  233.9 2.0 convolution_subtract_fusion.2
  236.9 16.3 %shard_map.91 = f32[128,128]{1,0:T(8,128)} custom-call(f32[128,128]{1,0:T(8,128)} %bitcast.157, f32[128,128]{1,0:T(8,128)} %convolution_add_fusion.8.right_ref.matrix_ref), custom_call_target="tpu_custom_call" | custom-call | tf_op jit(solution)/shard_map/pallas_call | solution.py:232
  253.3 2.6 convolution_add_fusion.6
  255.9 5.0 fusion.114
  262.3 25.7 %shard_map.92 = f32[32,4,128]{2,1,0:T(4,128)S(1)} custom-call(f32[32,4,128]{2,1,0:T(4,128)S(1)} %bitcast.144, bf16[1024,2048]{1,0:T(8,128)(2,1)S(1)} %copy-done.1, bf16[2048,1024]{1,0:T(8,128)(2,1)S(1)} %copy-done.4, bf16[2048,768]{1,0:T(8,128)(2,1)S(1)} %pad_maximum_fusion.refs_3_), custom_call_target="tpu_custom_call" | custom-call | tf_op jit(solution)/shard_map/pallas_call | solution.py:180
  289.6 3.9 fusion.3
  293.5 2.5 reduce_sum.246
  296.0 2.3 reshape.229
  298.3 3.1 fusion.130
  301.5 2.3 collective-permute-start.8
  305.2 6.0 %collective-permute-start.10 = (f32[128,384]{1,0:T(8,128)S(1)}, f32[128,384]{1,0:T(8,128)S(1)}, u32[]{:S(2)}, u32[]{:S(2)}) collective-permute-start(f32[128,384]{1,0:T(8,128)S(1)} %bitcast.175), channel_id=1, source_target_pairs={{0,8},{1,9},{2,10},{3,11},{4,12},{5,13},{6,14},{7,15},{8,16},{9,17... | collective-permute-start | bytes 589832 | tf_op jit(solution)/shard_map/ppermute | solution.py:244
  313.8 3.8 collective-permute-done.11
  317.8 3.8 fusion.2
  321.6 2.9 reduce_sum.247
  324.5 1.7 add.107
  329.2 28.5 %shard_map.93 = f32[32,4,384]{2,1,0:T(4,128)} custom-call(f32[32,4,384]{2,1,0:T(4,128)} %reshape.231.refs_0_), custom_call_target="tpu_custom_call" | custom-call | tf_op jit(solution)/shard_map/pallas_call | solution.py:106
  359.4 16.3 %shard_map.94 = f32[128,128]{1,0:T(8,128)} custom-call(f32[128,128]{1,0:T(8,128)} %slice.214.matrix_ref, f32[128,128]{1,0:T(8,128)} %convolution_add_fusion.8.right_ref.matrix_ref), custom_call_target="tpu_custom_call" | custom-call | tf_op jit(solution)/shard_map/pallas_call | solution.py:232
  375.7 1.7 fusion.93
  378.6 3.7 convolution_subtract_fusion.1
  383.3 16.4 %shard_map.95 = f32[128,128]{1,0:T(8,128)} custom-call(f32[128,128]{1,0:T(8,128)} %convolution_add_fusion.8.right_ref.matrix_ref, f32[128,128]{1,0:T(8,128)} %convolution_add_fusion.7.right_ref), custom_call_target="tpu_custom_call" | custom-call | tf_op jit(solution)/shard_map/pallas_call | solution.py:232
  399.7 2.6 convolution_add_fusion.4
  402.4 5.0 fusion.112
  407.8 2.0 convolution_add_fusion.5
  409.8 26.1 %shard_map.96 = f32[32,4,128]{2,1,0:T(4,128)S(1)} custom-call(f32[32,4,128]{2,1,0:T(4,128)S(1)} %bitcast.142, bf16[1024,2048]{1,0:T(8,128)(2,1)S(1)} %copy-done.2, bf16[2048,1024]{1,0:T(8,128)(2,1)S(1)} %copy-done.5, bf16[2048,768]{1,0:T(8,128)(2,1)S(1)} %pad_maximum_fusion.refs_3_), custom_call_target="tpu_custom_call" | custom-call | tf_op jit(solution)/shard_map/pallas_call | solution.py:180
  436.6 3.8 fusion.1
  440.4 1.7 reduce_sum.248
  443.2 3.6 fusion.129
  447.5 2.9 collective-permute-start.12
  451.7 22.6 %shard_map.97 = f32[32,4,128]{2,1,0:T(4,128)} custom-call(f32[32,4,128]{2,1,0:T(4,128)} %bitcast.166), custom_call_target="tpu_custom_call" | custom-call | tf_op jit(solution)/shard_map/pallas_call | solution.py:106
  474.3 16.3 %shard_map.98 = f32[128,128]{1,0:T(8,128)} custom-call(f32[128,128]{1,0:T(8,128)} %bitcast.165, f32[128,128]{1,0:T(8,128)} %convolution_add_fusion.7.right_ref), custom_call_target="tpu_custom_call" | custom-call | tf_op jit(solution)/shard_map/pallas_call | solution.py:232
  492.9 4.4 collective-permute-start.14
  498.6 2.9 fusion.20
  503.8 3.8 fusion
  507.6 1.9 reduce_sum.249
  509.6 2.0 fusion.19
  (220 shorter events, 65.1 us)
Async XLA Ops:
  3.2 169.0 %copy-start.39 = (s32[1536]{0:T(1024)}, s32[1536]{0:T(1024)S(1)}, u32[]{:S(2)}) copy-start(s32[1536]{0:T(1024)S(1)} %broadcast_select_fusion) | copy-start | bytes 18436
  11.8 20.5 %copy-start.42 = (s32[1,24]{1,0:T(1,128)S(1)}, s32[1,24]{1,0:T(1,128)}, u32[]{:S(2)}) copy-start(s32[1,24]{1,0:T(1,128)} %param.15) | copy-start | bytes 292
  13.4 47.1 %collective-permute-start = (f32[129,384]{1,0:T(8,128)}, f32[129,384]{1,0:T(8,128)}, u32[]{:S(2)}, u32[]{:S(2)}) collective-permute-start(f32[129,384]{1,0:T(8,128)} %bitcast.125), channel_id=1, source_target_pairs={{0,1},{1,2},{2,3},{3,4},{4,5},{5,6},{6,7},{7,8},{8,9},{9,10},{10,1... | collective-permute-start | bytes 594440 | tf_op jit(solution)/shard_map/ppermute | solution.py:244
  19.2 42.3 %collective-permute-start.1 = (f32[129,384]{1,0:T(8,128)}, f32[129,384]{1,0:T(8,128)}, u32[]{:S(2)}, u32[]{:S(2)}) collective-permute-start(f32[129,384]{1,0:T(8,128)} %bitcast.124), channel_id=1, source_target_pairs={{1,0},{2,1},{3,2},{4,3},{5,4},{6,5},{7,6},{8,7},{9,8},{10,9},{11,1... | collective-permute-start | bytes 594440 | tf_op jit(solution)/shard_map/ppermute | solution.py:244
  20.5 41.9 %collective-permute-start.2 = (f32[129,384]{1,0:T(8,128)S(1)}, f32[129,384]{1,0:T(8,128)}, u32[]{:S(2)}, u32[]{:S(2)}) collective-permute-start(f32[129,384]{1,0:T(8,128)S(1)} %bitcast.167), channel_id=1, source_target_pairs={{0,8},{1,9},{2,10},{3,11},{4,12},{5,13},{6,14},{7,15},{8,16},{9,17... | collective-permute-start | bytes 594440 | tf_op jit(solution)/shard_map/ppermute | solution.py:244
  28.9 34.5 %collective-permute-start.3 = (f32[129,384]{1,0:T(8,128)}, f32[129,384]{1,0:T(8,128)}, u32[]{:S(2)}, u32[]{:S(2)}) collective-permute-start(f32[129,384]{1,0:T(8,128)} %bitcast.126), channel_id=1, source_target_pairs={{8,0},{9,1},{10,2},{11,3},{12,4},{13,5},{14,6},{15,7},{16,8},{17,9... | collective-permute-start | bytes 594440 | tf_op jit(solution)/shard_map/ppermute | solution.py:244
  50.5 4.1 copy-start.33
  55.2 2.5 copy-start.38
  57.7 0.8 copy-start.18
  78.5 1.0 copy-start.6
  79.6 4.9 copy-start.23
  79.6 4.9 copy-start.19
  79.6 5.2 %copy-start = (bf16[1024,2048]{1,0:T(8,128)(2,1)S(1)}, bf16[1024,2048]{1,0:T(8,128)(2,1)}, u32[]{:S(2)}) copy-start(bf16[1024,2048]{1,0:T(8,128)(2,1)} %fusion.9.refs_1_) | copy-start | bytes 12582916
  79.6 6.2 %copy-start.3 = (bf16[2048,1024]{1,0:T(8,128)(2,1)S(1)}, bf16[2048,1024]{1,0:T(8,128)(2,1)}, u32[]{:S(2)}) copy-start(bf16[2048,1024]{1,0:T(8,128)(2,1)} %fusion.10.refs_2_) | copy-start | bytes 12582916
  126.1 17.1 %copy-start.7 = (f32[129,2048]{1,0:T(8,128)S(1)}, f32[129,2048]{1,0:T(8,128)}, u32[]{:S(2)}) copy-start(f32[129,2048]{1,0:T(8,128)} %copy-done.6) | copy-start | bytes 3170308
  126.1 18.7 %copy-start.24 = (bf16[128,2048]{1,0:T(8,128)(2,1)S(1)}, bf16[128,2048]{1,0:T(8,128)(2,1)}, u32[]{:S(2)}) copy-start(bf16[128,2048]{1,0:T(8,128)(2,1)} %copy-done.23) | copy-start | bytes 1572868
  126.1 18.7 %copy-start.25 = (f32[128,2048]{1,0:T(8,128)S(1)}, f32[128,2048]{1,0:T(8,128)}, u32[]{:S(2)}) copy-start(f32[128,2048]{1,0:T(8,128)} %get-tuple-element.73) | copy-start | bytes 3145732
  129.9 38.4 %collective-permute-start.4 = (f32[128,384]{1,0:T(8,128)}, f32[128,384]{1,0:T(8,128)}, u32[]{:S(2)}, u32[]{:S(2)}) collective-permute-start(f32[128,384]{1,0:T(8,128)} %bitcast.135), channel_id=1, source_target_pairs={{0,1},{1,2},{2,3},{3,4},{4,5},{5,6},{6,7},{7,8},{8,9},{9,10},{10,1... | collective-permute-start | bytes 589832 | tf_op jit(solution)/shard_map/ppermute | solution.py:244
  133.5 35.8 %collective-permute-start.5 = (f32[128,384]{1,0:T(8,128)}, f32[128,384]{1,0:T(8,128)}, u32[]{:S(2)}, u32[]{:S(2)}) collective-permute-start(f32[128,384]{1,0:T(8,128)} %bitcast.134), channel_id=1, source_target_pairs={{1,0},{2,1},{3,2},{4,3},{5,4},{6,5},{7,6},{8,7},{9,8},{10,9},{11,1... | collective-permute-start | bytes 589832 | tf_op jit(solution)/shard_map/ppermute | solution.py:244
  134.8 35.4 %collective-permute-start.6 = (f32[128,384]{1,0:T(8,128)S(1)}, f32[128,384]{1,0:T(8,128)}, u32[]{:S(2)}, u32[]{:S(2)}) collective-permute-start(f32[128,384]{1,0:T(8,128)S(1)} %bitcast.172), channel_id=1, source_target_pairs={{0,8},{1,9},{2,10},{3,11},{4,12},{5,13},{6,14},{7,15},{8,16},{9,17... | collective-permute-start | bytes 589832 | tf_op jit(solution)/shard_map/ppermute | solution.py:244
  141.9 29.3 %collective-permute-start.7 = (f32[128,384]{1,0:T(8,128)}, f32[128,384]{1,0:T(8,128)}, u32[]{:S(2)}, u32[]{:S(2)}) collective-permute-start(f32[128,384]{1,0:T(8,128)} %bitcast.138), channel_id=1, source_target_pairs={{8,0},{9,1},{10,2},{11,3},{12,4},{13,5},{14,6},{15,7},{16,8},{17,9... | collective-permute-start | bytes 589832 | tf_op jit(solution)/shard_map/ppermute | solution.py:244
  178.9 2.8 copy-start.8
  180.6 2.1 copy-start.16
  228.4 5.1 %copy-start.31 = (f32[128,128]{1,0:T(8,128)S(1)}, f32[128,128]{1,0:T(8,128)}, u32[]{:S(2)}) copy-start(f32[128,128]{1,0:T(8,128)} %shard_map.90) | copy-start | bytes 196612
  228.4 5.4 %copy-start.9 = (f32[129,2048]{1,0:T(8,128)S(1)}, f32[129,2048]{1,0:T(8,128)}, u32[]{:S(2)}) copy-start(f32[129,2048]{1,0:T(8,128)} %copy-done.6) | copy-start | bytes 3170308
  228.5 5.4 %copy-start.17 = (f32[128,2048]{1,0:T(8,128)S(1)}, f32[128,2048]{1,0:T(8,128)}, u32[]{:S(2)}) copy-start(f32[128,2048]{1,0:T(8,128)} %copy-done.16) | copy-start | bytes 3145732
  231.9 4.1 copy-start.34
  233.9 2.1 copy-start.36
  255.9 5.1 copy-start.10
  255.9 5.1 copy-start.20
  255.9 5.4 %copy-start.1 = (bf16[1024,2048]{1,0:T(8,128)(2,1)S(1)}, bf16[1024,2048]{1,0:T(8,128)(2,1)}, u32[]{:S(2)}) copy-start(bf16[1024,2048]{1,0:T(8,128)(2,1)} %fusion.9.refs_1_) | copy-start | bytes 12582916
  255.9 6.4 %copy-start.4 = (bf16[2048,1024]{1,0:T(8,128)(2,1)S(1)}, bf16[2048,1024]{1,0:T(8,128)(2,1)}, u32[]{:S(2)}) copy-start(bf16[2048,1024]{1,0:T(8,128)(2,1)} %fusion.10.refs_2_) | copy-start | bytes 12582916
  288.0 1.6 copy-start.40
  298.3 14.2 %copy-start.11 = (f32[128,2048]{1,0:T(8,128)S(1)}, f32[128,2048]{1,0:T(8,128)}, u32[]{:S(2)}) copy-start(f32[128,2048]{1,0:T(8,128)} %copy-done.10) | copy-start | bytes 3145732
  298.3 14.2 %copy-start.26 = (f32[128,2048]{1,0:T(8,128)S(1)}, f32[128,2048]{1,0:T(8,128)}, u32[]{:S(2)}) copy-start(f32[128,2048]{1,0:T(8,128)} %get-tuple-element.74) | copy-start | bytes 3145732
  301.5 11.7 %collective-permute-start.8 = (f32[128,384]{1,0:T(8,128)S(1)}, f32[128,384]{1,0:T(8,128)S(1)}, u32[]{:S(2)}, u32[]{:S(2)}) collective-permute-start(f32[128,384]{1,0:T(8,128)S(1)} %bitcast.178), channel_id=1, source_target_pairs={{0,1},{1,2},{2,3},{3,4},{4,5},{5,6},{6,7},{7,8},{8,9},{9,10},{10,1... | collective-permute-start | bytes 589832 | tf_op jit(solution)/shard_map/ppermute | solution.py:244
  303.8 9.4 %collective-permute-start.9 = (f32[128,384]{1,0:T(8,128)S(1)}, f32[128,384]{1,0:T(8,128)S(1)}, u32[]{:S(2)}, u32[]{:S(2)}) collective-permute-start(f32[128,384]{1,0:T(8,128)S(1)} %bitcast.179), channel_id=1, source_target_pairs={{1,0},{2,1},{3,2},{4,3},{5,4},{6,5},{7,6},{8,7},{9,8},{10,9},{11,1... | collective-permute-start | bytes 589832 | tf_op jit(solution)/shard_map/ppermute | solution.py:244
  305.2 8.6 %collective-permute-start.10 = (f32[128,384]{1,0:T(8,128)S(1)}, f32[128,384]{1,0:T(8,128)S(1)}, u32[]{:S(2)}, u32[]{:S(2)}) collective-permute-start(f32[128,384]{1,0:T(8,128)S(1)} %bitcast.175), channel_id=1, source_target_pairs={{0,8},{1,9},{2,10},{3,11},{4,12},{5,13},{6,14},{7,15},{8,16},{9,17... | collective-permute-start | bytes 589832 | tf_op jit(solution)/shard_map/ppermute | solution.py:244
  311.2 6.4 %collective-permute-start.11 = (f32[128,384]{1,0:T(8,128)S(1)}, f32[128,384]{1,0:T(8,128)S(1)}, u32[]{:S(2)}, u32[]{:S(2)}) collective-permute-start(f32[128,384]{1,0:T(8,128)S(1)} %bitcast.176), channel_id=1, source_target_pairs={{8,0},{9,1},{10,2},{11,3},{12,4},{13,5},{14,6},{15,7},{16,8},{17,9... | collective-permute-start | bytes 589832 | tf_op jit(solution)/shard_map/ppermute | solution.py:244
  324.5 2.8 copy-start.22
  326.2 1.1 copy-start.15
  329.2 53.2 %copy-start.32 = (f32[128,128]{1,0:T(8,128)S(1)}, f32[128,128]{1,0:T(8,128)}, u32[]{:S(2)}) copy-start(f32[128,128]{1,0:T(8,128)} %convolution_add_fusion.8.right_ref.matrix_ref) | copy-start | bytes 196612
  375.7 6.7 %copy-start.30 = (f32[128,128]{1,0:T(8,128)S(1)}, f32[128,128]{1,0:T(8,128)}, u32[]{:S(2)}) copy-start(f32[128,128]{1,0:T(8,128)} %shard_map.94) | copy-start | bytes 196612
  378.6 3.8 copy-start.37
  402.3 5.1 copy-start.13
  402.3 5.1 copy-start.21
  402.3 5.4 %copy-start.12 = (f32[128,2048]{1,0:T(8,128)S(1)}, f32[128,2048]{1,0:T(8,128)}, u32[]{:S(2)}) copy-start(f32[128,2048]{1,0:T(8,128)} %copy-done.10) | copy-start | bytes 3145732
  402.4 5.4 %copy-start.29 = (f32[128,2048]{1,0:T(8,128)S(1)}, f32[128,2048]{1,0:T(8,128)}, u32[]{:S(2)}) copy-start(f32[128,2048]{1,0:T(8,128)} %fusion.62) | copy-start | bytes 3145732
  402.4 7.4 %copy-start.5 = (bf16[2048,1024]{1,0:T(8,128)(2,1)S(1)}, bf16[2048,1024]{1,0:T(8,128)(2,1)}, u32[]{:S(2)}) copy-start(bf16[2048,1024]{1,0:T(8,128)(2,1)} %fusion.10.refs_2_) | copy-start | bytes 12582916
  407.4 2.4 copy-start.2
  435.9 0.7 copy-start.41
  440.4 10.0 %copy-start.14 = (f32[128,2048]{1,0:T(8,128)S(1)}, f32[128,2048]{1,0:T(8,128)}, u32[]{:S(2)}) copy-start(f32[128,2048]{1,0:T(8,128)} %copy-done.13) | copy-start | bytes 3145732
  446.8 51.8 %copy-start.28 = (f32[128,2048]{1,0:T(8,128)S(1)}, f32[128,2048]{1,0:T(8,128)}, u32[]{:S(2)}) copy-start(f32[128,2048]{1,0:T(8,128)} %convolution_add_fusion.5) | copy-start | bytes 3145732
  447.5 54.0 %collective-permute-start.12 = (f32[128,384]{1,0:T(8,128)}, f32[128,384]{1,0:T(8,128)}, u32[]{:S(2)}, u32[]{:S(2)}) collective-permute-start(f32[128,384]{1,0:T(8,128)} %bitcast.129), channel_id=1, source_target_pairs={{0,1},{1,2},{2,3},{3,4},{4,5},{5,6},{6,7},{7,8},{8,9},{9,10},{10,1... | collective-permute-start | bytes 589832 | tf_op jit(solution)/shard_map/ppermute | solution.py:244
  491.5 10.9 %collective-permute-start.13 = (f32[128,384]{1,0:T(8,128)S(1)}, f32[128,384]{1,0:T(8,128)S(1)}, u32[]{:S(2)}, u32[]{:S(2)}) collective-permute-start(f32[128,384]{1,0:T(8,128)S(1)} %bitcast.177), channel_id=1, source_target_pairs={{1,0},{2,1},{3,2},{4,3},{5,4},{6,5},{7,6},{8,7},{9,8},{10,9},{11,1... | collective-permute-start | bytes 589832 | tf_op jit(solution)/shard_map/ppermute | solution.py:244
  492.9 9.6 %collective-permute-start.14 = (f32[128,384]{1,0:T(8,128)S(1)}, f32[128,384]{1,0:T(8,128)S(1)}, u32[]{:S(2)}, u32[]{:S(2)}) collective-permute-start(f32[128,384]{1,0:T(8,128)S(1)} %bitcast.173), channel_id=1, source_target_pairs={{0,8},{1,9},{2,10},{3,11},{4,12},{5,13},{6,14},{7,15},{8,16},{9,17... | collective-permute-start | bytes 589832 | tf_op jit(solution)/shard_map/ppermute | solution.py:244
  497.3 6.4 %collective-permute-start.15 = (f32[128,384]{1,0:T(8,128)S(1)}, f32[128,384]{1,0:T(8,128)S(1)}, u32[]{:S(2)}, u32[]{:S(2)}) collective-permute-start(f32[128,384]{1,0:T(8,128)S(1)} %bitcast.174), channel_id=1, source_target_pairs={{8,0},{9,1},{10,2},{11,3},{12,4},{13,5},{14,6},{15,7},{16,8},{17,9... | collective-permute-start | bytes 589832 | tf_op jit(solution)/shard_map/ppermute | solution.py:244
  507.6 1.9 copy-start.27
  507.6 1.9 copy-start.35

commit v2 on v0

v2 whole, which is shorter than its diff:
```python
import jax
import jax.numpy as jnp
from jax import lax
from jax.experimental import pallas as pl
from jax.experimental.pallas import tpu as pltpu
from jax.sharding import PartitionSpec as P

ITERS = 3
HIGH = lax.Precision.HIGHEST
MESH = pl.DeviceIdType.MESH
F32, BF16, I32 = jnp.float32, jnp.bfloat16, jnp.int32
VMEM = pl.BlockSpec(memory_space=pltpu.VMEM)
TILE = 256
LANES = 128


def high_and_rest(values):
    first = values.astype(BF16).astype(F32)
    return first, values - first


def nt(left, right, precision=None):
    return lax.dot_general(
        left, right, (((1,), (1,)), ((), ())), preferred_element_type=F32, precision=precision
    )


def nn(left, right, precision=None):
    return jnp.dot(left, right, preferred_element_type=F32, precision=precision)


def lanes(step, size):
    return pl.ds(pl.multiple_of(step * size, size), size)


def loop(count, body):
    def one(step, carry):
        body(step)
        return carry

    lax.fori_loop(0, count, one, 0)


def greet(groups):
    barrier = pltpu.get_barrier_semaphore()
    for axis, count in groups:
        me = lax.axis_index(axis)

        def one(step, carry, axis=axis, count=count, me=me):
            pl.semaphore_signal(
                barrier,
                inc=1,
                device_id={axis: lax.rem(me + step, count)},
                device_id_type=MESH,
            )
            return carry

        lax.fori_loop(1, count, one, 0)
    pl.semaphore_wait(barrier, sum(count - 1 for _, count in groups))


def send_all(axis, count, pick, landing, sems):
    me = lax.axis_index(axis)

    def one(step, carry):
        peer = lax.rem(me + step, count)
        pltpu.make_async_remote_copy(
            src_ref=pick(peer),
            dst_ref=landing.at[me],
            send_sem=sems.at[0],
            recv_sem=sems.at[1],
            device_id={axis: peer},
            device_id_type=MESH,
        ).start()
        return carry

    lax.fori_loop(1, count, one, 0)


def wait_all(count, landing, sems):
    whole = landing.at[pl.ds(0, count - 1)]
    pltpu.make_async_copy(whole, whole, sems.at[1]).wait()
    pltpu.make_async_copy(whole, whole, sems.at[0]).wait()


def sum_slots(count, landing):
    total = landing[0]
    for slot in range(1, count):
        total = total + landing[slot]
    return total


def stacked_dot(rows, matrix, dot):
    first, rest = high_and_rest(rows)
    second, third = high_and_rest(rest)
    stack = jnp.concatenate([first, second, third, jnp.zeros_like(rows)], axis=0).astype(BF16)
    full = dot(stack, matrix)
    return full[0:4] + full[4:8] + full[8:12]


def eliminate(work, first, last):
    size = work.shape[0]
    row_at = lax.broadcasted_iota(I32, (8, 1), 0)

    def block(step, carry):
        at = pl.ds(pl.multiple_of(step * 8, 8), 8)
        panel = work[at, :]
        for k in range(8):
            row = panel[k : k + 1, :]
            row = row * (1.0 / row[:, k : k + 1])
            panel = jnp.where(row_at == k, row, panel - panel[:, k : k + 1] * row)
        full = work[...]
        left, right = full[:, 0:size], full[:, size:]
        for k in range(8):
            column = full[:, k : k + 1]
            left = left - column * panel[k : k + 1, 0:size]
            right = right - column * panel[k : k + 1, size:]
        work[:, 0:size] = pltpu.roll(left, size - 8, 1)
        work[:, size:] = right
        work[at, 0:size] = pltpu.roll(panel[:, 0:size], size - 8, 1)
        work[at, size:] = panel[:, size:]
        return carry

    lax.fori_loop(first, last, block, 0)


def body(
    n_sub, n_coarse,
    operator, coupling, coarse_rows, loads, lists, maps,
    solution, residual,
    hot, spread, pick, inverse, near, direction, rounded, product, image, pieces,
    face_out, face_in, invd, scaled, gram, blend, picked, terms_mine,
    terms, terms_in, part_rows, part_in, solved_rows, solved_in, picks, picks_in,
    sums, sums_in, mid_rows, mid_in, sums_out, maps_in, solver, inverter, sems, face_sems,
):
    me, group = lax.axis_index("sub"), lax.axis_index("coarse")
    height, width = loads.shape
    corners = coupling.shape[0]
    slots = hot.shape[1]
    span = slots // 4
    row_length = n_sub // 4
    tiles = n_sub // 4
    column, row = lax.rem(me, row_length), me // row_length
    sides = (
        (-1, column > 0),
        (1, column < row_length - 1),
        (-row_length, row > 0),
        (row_length, row < 3),
    )

    def faces_start(rows):
        for face, (shift, there) in enumerate(sides):
            other = face ^ 1

            @pl.when(there)
            def _(face=face, shift=shift, other=other):
                pltpu.make_async_remote_copy(
                    src_ref=face_out.at[pl.ds(0, rows), pl.ds(face * span, span)],
                    dst_ref=face_in.at[pl.ds(0, rows), pl.ds(other * span, span)],
                    send_sem=face_sems.at[0, face],
                    recv_sem=face_sems.at[1, other],
                    device_id={"sub": me + shift},
                    device_id_type=MESH,
                ).start()

    def faces_wait(rows):
        for face, (_, there) in enumerate(sides):

            @pl.when(there)
            def _(face=face):
                view = face_in.at[pl.ds(0, rows), pl.ds(face * span, span)]
                pltpu.make_async_copy(view, view, face_sems.at[1, face]).wait()
                pltpu.make_async_copy(view, view, face_sems.at[0, face]).wait()

    def gather(rows):
        def one(step):
            at = lanes(step, TILE)
            full = nn(pieces[0 : 2 * rows, :], hot[:, at])
            face_out[0:rows, at] = full[0:rows] + full[rows : 2 * rows]

        loop(slots // TILE, one)

    def scatter_rows(rows, store):
        first, rest = high_and_rest(face_in[0:rows, :])
        pieces[0:rows, 0:slots] = first.astype(BF16)
        pieces[rows : 2 * rows, 0:slots] = rest.astype(BF16)

        def one(step):
            at = lanes(step, TILE)
            full = nt(pieces[0 : 2 * rows, 0:slots], hot[at, :])
            store(at, full[0:rows] + full[rows : 2 * rows])

        loop(width // TILE, one)

    def all_sum_start():
        sums_in[me] = sums[me]
        send_all("sub", n_sub, lambda peer: sums.at[peer], sums_in, sems.at[4])

    def all_sum_finish():
        wait_all(n_sub, sums_in, sems.at[4])
        partial = sum_slots(n_sub, sums_in)
        mid_rows[...] = partial
        mid_in[group] = partial
        send_all("coarse", n_coarse, lambda peer: mid_rows, mid_in, sems.at[5])
        wait_all(n_coarse, mid_in, sems.at[5])
        total = sum_slots(n_coarse, mid_in)
        mid_rows[...] = total
        sums_out[me] = total
        send_all("sub", n_sub, lambda peer: mid_rows, sums_out, sems.at[6])
        wait_all(n_sub, sums_out, sems.at[6])

    face_in[...] = jnp.zeros_like(face_in)
    greet((("sub", n_sub), ("coarse", n_coarse)))
    maps_in[me] = maps[...]
    send_all("sub", n_sub, lambda peer: maps, maps_in, sems.at[7])

    def build_hot(step):
        at = lanes(step, LANES)
        index = lax.broadcasted_iota(I32, (width, LANES), 0)
        hot[:, at] = jnp.where(index == lists[:, at], 1.0, 0.0).astype(BF16)

    loop(slots // LANES, build_hot)
    eye = lax.broadcasted_iota(I32, (LANES, LANES), 0) == lax.broadcasted_iota(
        I32, (LANES, LANES), 1
    )
    face_rows = height + 8 + corners
    image[...] = jnp.zeros_like(image)
    for at in range(0, width, LANES):
        block = operator[at : at + LANES, at : at + LANES].astype(F32)
        image[0:1, at : at + LANES] = jnp.sum(jnp.where(eye, block, 0.0), axis=0, keepdims=True)
    values = jnp.concatenate([loads[...], image[0:8, :], coupling[...]], axis=0)
    first, rest = high_and_rest(values)
    pieces[0:face_rows, :] = first.astype(BF16)
    pieces[face_rows : 2 * face_rows, :] = rest.astype(BF16)
    gather(face_rows)
    faces_start(face_rows)
    rows_of = coarse_rows.shape[0]
    first, rest = high_and_rest(coarse_rows[...])
    inverse[...] = jnp.zeros_like(inverse)
    inverse[0:rows_of, :] = first.astype(BF16)
    inverse[256 : 256 + rows_of, :] = rest.astype(BF16)
    wait_all(n_sub, maps_in, sems.at[7])
    for t in range(tiles):
        both = sum_slots(4, maps_in.at[pl.ds(4 * t, 4)])
        at = slice(LANES * t, LANES * (t + 1))
        index = lax.broadcasted_iota(I32, (spread.shape[0], LANES), 0) + 1
        spread[:, at] = jnp.where(index == both[0:1, :], 1.0, 0.0).astype(BF16)
        index = lax.broadcasted_iota(I32, (pick.shape[0], LANES), 0) + 1
        pick[:, at] = jnp.where(index == both[1:2, :], 1.0, 0.0).astype(BF16)
    faces_wait(face_rows)

    product[...] = jnp.zeros_like(product)
    for face in range(4):
        at = slice(face * span, (face + 1) * span)
        product[corners * (face + 1) : corners * (face + 2), at] = face_in[height + 8 : face_rows, at]
    rounded[...] = product[...].astype(BF16)

    def build_near(step):
        at = lanes(step, TILE)
        tile = nt(rounded[:, 0:slots], hot[at, :])
        both = jnp.concatenate([coupling[:, at], tile[corners:]], axis=0)
        near[:, at] = both.astype(BF16)

    loop(width // TILE, build_near)

    rows = height + 16

    def finish_setup(at, added):
        combined = loads[:, at] + added[0:height]
        diagonal = image[0:1, at] + added[height : height + 1]
        residual[:, at] = combined
        invd[:, at] = 1.0 / diagonal
        direction[:, at] = combined / diagonal
        rounded[:, at] = direction[:, at].astype(BF16)
        solution[:, at] = jnp.zeros_like(combined)

    ones = jnp.ones((16, slots), BF16)

    def build_weight(step):
        at = lanes(step, TILE)
        scaled[:, at] = 1.0 / (1.0 + nt(ones, hot[at, :])[0:1])

    loop(width // TILE, build_weight)
    scatter_rows(rows, finish_setup)
    scaled[...] = scaled[...] * invd[...]
    start = nt(residual[...] * scaled[...], residual[...], HIGH)
    sums[...] = jnp.zeros_like(sums)
    for p in range(n_sub):
        sums[p, :, 0:LANES] = start[4 * p : 4 * p + 4, :]
    all_sum_start()
    all_sum_finish()
    for p in range(n_sub):
        gram[4 * p : 4 * p + 4, :] = sums_out[p, :, 0:LANES]

    lane_at = lax.broadcasted_iota(I32, (8, LANES), 1)
    own_lanes = lax.broadcasted_iota(I32, (height, LANES), 1) < corners
    slot_of = lax.rem(me, 4)

    def iteration(turn):
        mine = jnp.where(own_lanes, nt(rounded[...], near[...]), 0.0)
        terms_mine[...] = mine
        placed = mine
        for q in range(1, 4):
            placed = jnp.where(slot_of == q, pltpu.roll(mine, 32 * q, 1), placed)
        for p in range(n_sub):
            terms[p] = placed[4 * p : 4 * p + 4, :]
        terms_in[me] = terms[me]
        send_all("sub", n_sub, lambda peer: terms.at[peer], terms_in, sems.at[0])

        def multiply(step):
            at = lanes(step, TILE)
            tile = nn(rounded[...], operator[:, at])
            product[:, at] = tile
            first, rest = high_and_rest(tile)
            pieces[0:height, at] = first.astype(BF16)
            pieces[height : 2 * height, at] = rest.astype(BF16)

        loop(width // TILE, multiply)
        wait_all(n_sub, terms_in, sems.at[0])
        row_tiles = [sum_slots(4, terms_in.at[pl.ds(4 * t, 4)]) for t in range(tiles)]
        partial = stacked_dot(jnp.concatenate(row_tiles, axis=1), spread[...], nt)
        part_rows[...] = partial
        part_in[group] = partial
        send_all("coarse", n_coarse, lambda peer: part_rows, part_in, sems.at[1])
        gather(height)
        faces_start(height)
        wait_all(n_coarse, part_in, sems.at[1])
        wide = stacked_dot(sum_slots(n_coarse, part_in), inverse[...], nt)
        solved = wide[:, 0:256] + wide[:, 256:512]
        solved_rows[...] = solved
        solved_in[group] = solved
        send_all("coarse", n_coarse, lambda peer: solved_rows, solved_in, sems.at[2])
        both = nt(rounded[...], pieces[0 : 2 * height, :])
        curvature = both[:, 0:height] + both[:, height : 2 * height]
        inverter[:, 0:height] = gram[...]
        inverter[:, height:] = jnp.where(eye, 1.0, 0.0)
        eliminate(inverter, 0, 4)
        wait_all(n_coarse, solved_in, sems.at[2])
        everything = jnp.concatenate([solved_in[c] for c in range(n_coarse)], axis=1)
        chosen = stacked_dot(everything, pick[...], nn)
        doubled = jnp.concatenate([chosen, chosen], axis=0)
        for peer in range(n_sub):
            at_row, at_column = divmod(peer, row_length)
            sources = [(peer, 0)]
            if at_column > 0:
                sources.append((peer - 1, 1))
            if at_column < row_length - 1:
                sources.append((peer + 1, 2))
            if at_row > 0:
                sources.append((peer - row_length, 3))
            if at_row < 3:
                sources.append((peer + row_length, 4))
            total = jnp.zeros((8, LANES), F32)
            for source, place in sources:
                t = source // 4
                tile = doubled[:, LANES * t : LANES * (t + 1)]
                shift = (corners * place - 32 * (source % 4)) % LANES
                if shift:
                    tile = pltpu.roll(tile, shift, 1)
                here = (lane_at >= corners * place) & (lane_at < corners * (place + 1))
                total = jnp.where(here, tile, total)
            picks[peer] = total[0:4]
        picks_in[me] = picks[me]
        send_all("sub", n_sub, lambda peer: picks.at[peer], picks_in, sems.at[3])
        faces_wait(height)

        def add_faces(at, added):
            image[:, at] = product[:, at] + added

        scatter_rows(height, add_faces)
        eliminate(inverter, 4, 8)
        wait_all(n_sub, picks_in, sems.at[3])
        for p in range(n_sub):
            picked[4 * p : 4 * p + 4, :] = picks_in[p]
        curvature = curvature + nt(
            terms_mine[...], jnp.where(own_lanes, picked[...], 0.0), HIGH
        )
        first, rest = high_and_rest(picked[...])
        stack = jnp.concatenate([first, rest], axis=0).astype(BF16)

        def add_corners(step):
            at = lanes(step, TILE)
            full = nn(stack, near[:, at])
            image[:, at] = image[:, at] + full[0:height] + full[height : 2 * height]

        loop(width // TILE, add_corners)
        weighted = image[...] * scaled[...]
        mixed = nt(weighted, residual[...], HIGH)
        square = nt(weighted, image[...], HIGH)
        for p in range(n_sub):
            part = slice(4 * p, 4 * p + 4)
            sums[p, :, 0:LANES] = curvature[part, :]
            sums[p, :, LANES : 2 * LANES] = mixed[part, :]
            sums[p, :, 2 * LANES : 3 * LANES] = square[part, :]
        all_sum_start()
        eliminate(inverter, 8, 16)
        all_sum_finish()
        for p in range(n_sub):
            part = slice(4 * p, 4 * p + 4)
            solver[part, 0:LANES] = sums_out[p, :, 0:LANES]
        solver[:, height:] = gram[...]
        eliminate(solver, 0, height // 8)
        step_size = solver[:, height:]
        step_turned = step_size.T

        @pl.when(turn < ITERS - 1)
        def _():
            for p in range(n_sub):
                part = slice(4 * p, 4 * p + 4)
                solver[part, :] = sums_out[p, :, LANES : 3 * LANES]
            cross = nn(step_turned, solver[:, 0:LANES], HIGH)
            twice = nn(step_turned, nn(solver[:, LANES:], step_size, HIGH), HIGH)
            fresh = gram[...] - cross - cross.T + twice
            blend[...] = nn(fresh, inverter[:, height:], HIGH)
            gram[...] = fresh

        factors = jnp.concatenate([step_turned, blend[...]], axis=0)

        def update(step):
            at = lanes(step, TILE)
            moved = nn(factors, direction[:, at], HIGH)
            solution[:, at] = solution[:, at] + moved[0:height]
            left = residual[:, at] - nn(step_turned, image[:, at], HIGH)
            residual[:, at] = left
            ahead = left * invd[:, at] + moved[height : 2 * height]
            direction[:, at] = ahead
            rounded[:, at] = ahead.astype(BF16)

        loop(width // TILE, update)

    blend[...] = jnp.zeros_like(blend)
    loop(ITERS, iteration)


def local(
    local_operators, couplings, coarse_inverse, local_loads, face_lists, face_counts, corner_map
):
    slot_lists = face_lists[0]
    face_total, slot_total = slot_lists.shape
    _, height, width = local_loads.shape
    corners = couplings.shape[1]
    n_sub, n_coarse = lax.axis_size("sub"), lax.axis_size("coarse")
    slots = face_total * slot_total
    rows, coarse_total = coarse_inverse.shape
    face_rows = height + 8 + corners
    split = n_sub // 4 * LANES

    usable = lax.broadcasted_iota(I32, (face_total, slot_total), 1) < face_counts[0][:, None]
    marked = jnp.where(usable, slot_lists, -1).reshape(1, slots)
    place = corner_map // rows * 256 + corner_map % rows
    both = jnp.concatenate([corner_map, place], axis=0) + 1
    maps = lax.dynamic_update_slice(
        jnp.zeros((2, LANES), I32), both, (0, lax.rem(lax.axis_index("sub"), 4) * 32)
    )
    result = [jax.ShapeDtypeStruct((height, width), F32)] * 2
    per = height // n_sub
    scratch = [
        pltpu.VMEM((width, slots), BF16),
        pltpu.VMEM((coarse_total, split), BF16),
        pltpu.VMEM((n_coarse * 256, split), BF16),
        pltpu.VMEM((512, coarse_total), BF16),
        pltpu.VMEM((LANES, width), BF16),
        pltpu.VMEM((height, width), F32),
        pltpu.VMEM((height, width), BF16),
        pltpu.VMEM((height, width), F32),
        pltpu.VMEM((height, width), F32),
        pltpu.VMEM((2 * face_rows, width), BF16),
        pltpu.VMEM((face_rows, slots), F32),
        pltpu.VMEM((face_rows, slots), F32),
        pltpu.VMEM((1, width), F32),
        pltpu.VMEM((1, width), F32),
        pltpu.VMEM((height, height), F32),
        pltpu.VMEM((height, height), F32),
        pltpu.VMEM((height, LANES), F32),
        pltpu.VMEM((height, LANES), F32),
        pltpu.VMEM((n_sub, per, LANES), F32),
        pltpu.VMEM((n_sub, per, LANES), F32),
        pltpu.VMEM((per, coarse_total), F32),
        pltpu.VMEM((n_coarse, per, coarse_total), F32),
        pltpu.VMEM((per, 256), F32),
        pltpu.VMEM((n_coarse, per, 256), F32),
        pltpu.VMEM((n_sub, per, LANES), F32),
        pltpu.VMEM((n_sub, per, LANES), F32),
        pltpu.VMEM((n_sub, per, 3 * height), F32),
        pltpu.VMEM((n_sub, per, 3 * height), F32),
        pltpu.VMEM((per, 3 * height), F32),
        pltpu.VMEM((n_coarse, per, 3 * height), F32),
        pltpu.VMEM((n_sub, per, 3 * height), F32),
        pltpu.VMEM((n_sub, 2, LANES), I32),
        pltpu.VMEM((height, 2 * height), F32),
        pltpu.VMEM((height, 2 * height), F32),
        pltpu.SemaphoreType.DMA((8, 2)),
        pltpu.SemaphoreType.DMA((2, 4)),
    ]
    solved, left = pl.pallas_call(
        lambda *refs: body(n_sub, n_coarse, *refs),
        out_shape=result,
        in_specs=[VMEM] * 6,
        out_specs=[VMEM] * 2,
        scratch_shapes=scratch,
        compiler_params=pltpu.CompilerParams(
            collective_id=0, has_side_effects=True, vmem_limit_bytes=60 << 20
        ),
    )(local_operators[0], couplings[0].astype(F32), coarse_inverse, local_loads[0], marked, maps)
    return (solved[None], left[None])


def solution(mesh):
    return jax.shard_map(
        local,
        mesh=mesh,
        in_specs=(
            P(("coarse", "sub"), None, None),
            P(("coarse", "sub"), None, None),
            P("coarse", None),
            P(("coarse", "sub"), None, None),
            P(("coarse", "sub"), None, None),
            P(("coarse", "sub"), None),
            P(("coarse", "sub"), None),
        ),
        out_specs=(P(("coarse", "sub"), None, None), P(("coarse", "sub"), None, None)),
        check_vma=False,
    )
```

time: 1920 us -> 265 us (0.14)
  waiting for transfers between devices: 1320 us -> 0 us
  other arithmetic: 270 us -> 4.25 us
  Pallas kernels: 0 us -> 255 us
  blocking collectives: 120 us -> 0 us
  matrix products: 69.5 us -> 0 us
  local copies, waits for them, and re-layouts: 69.1 us -> 5.46 us
  starting transfers between devices: 43.6 us -> 0 us
    psum x5 -> x0, waiting for transfers between devices: 1120 us -> none  [the longest x3 678 us: gram(): lax.psum(jnp.einsum('lm,km->lk', leading_part * weight, trailing_part, pr...]
    pallas_call x0 -> x1, Pallas kernels: none -> 255 us  [local(): pl.pallas_call(lambda *refs: body(n_sub, n_coarse, *refs), out_shape=resu...]
    all_gather x3 -> x0, waiting for transfers between devices: 186 us -> none  [local(): lax.all_gather(corner_terms, ('coarse', 'sub'), axis=1, tiled=True)]
    scatter-add x8 -> x0, other arithmetic: 140 us -> none  [the longest x3 92.1 us: local(): jnp.zeros((loads, coarse_total), jnp.float32).at[:, every_corner]]
    all_gather x4 -> x0, blocking collectives: 120 us -> none  [the longest x1 78.4 us: local(): lax.all_gather(corner_index, ('coarse', 'sub'), axis=0, tiled=True)]
    another operation x29 -> x0, other arithmetic: 119 us -> none  [the longest x15 62.1 us: spd_solve(): factor = jnp.linalg.cholesky(matrix)]
    dot_general x32 -> x0, matrix products: 64.5 us -> none  [the longest x3 16.9 us: local(): jnp.dot(rounded, operator_block, preferred_element_type=jnp.float32)]
    gather x8 -> x0, local copies, waits for them, and re-layouts: 47.2 us -> none  [the longest x1 32 us: local(): diagonal = jnp.diagonal(operator_block).astype(jnp.float32)[None]]
  transfers between devices with their start and end apart: 24 -> 0, of which waited for: 10 -> 0; matrix products, arithmetic and copies ran while one was open for 9% -> 0% of each run, Pallas kernels for 0% -> 0%
where the time goes in v2:
time: 265 us
  Pallas kernels  255 us (96%)
  local copies, waits for them, and re-layouts  5.46 us (2%)
  other arithmetic  4.25 us (2%)
    pallas_call x1, Pallas kernels, local(): pl.pallas_call(lambda *refs: body(n_sub, n_coarse, *refs), out_shape=resu...  255 us
    unnamed x6, local copies, waits for them, and re-layouts  5.31 us

profile of v2, /device:TPU:1, one launch (start us, length us, event | category | flops | bytes accessed | tf_op | source)
XLA Modules:
  0.0 265.1 jit_solution(6999453491214577480)
XLA Ops:
  0.6 0.7 fusion.1
  1.3 0.7 add_add_fusion
  2.0 0.1 dynamic_update_slice.3.refs_5_
  2.1 0.0 copy-start
  2.1 0.7 fusion
  2.9 0.7 copy.10
  3.6 0.6 broadcast_select_fusion.refs_4_
  4.2 1.6 bitcast_convert_fusion.refs_1_
  5.8 0.0 copy-done
  5.8 254.8 %shard_map.86 = (f32[128,2048]{1,0:T(8,128)}, f32[128,2048]{1,0:T(8,128)}) custom-call(bf16[2048,2048]{1,0:T(8,128)(2,1)} %bitcast.14, f32[24,2048]{1,0:T(8,128)} %bitcast_convert_fusion.refs_1_, f32[192,1536]{1,0:T(8,128)} %refs_2_.1, f32[128,2048]{1,0:T(8,128)} %bitcast.15, s32[1,1536]{1,0:T(1,128)} %broadcast_select_fusion.refs_4_, s32[2,128]{1,0:T(2,128)} %copy-done), custom_call_target="tpu_custom_call" | custom-call | tf_op jit(solution)/shard_map/pallas_call | solution.py:495
  260.6 2.3 copy.14
  262.9 2.3 copy.15
  (2 shorter events, 0.0 us)
Async XLA Ops:
  2.1 3.6 %copy-start = (s32[2,128]{1,0:T(2,128)}, s32[2,128]{1,0:T(2,128)S(1)}, u32[]{:S(2)}) copy-start(s32[2,128]{1,0:T(2,128)S(1)} %dynamic_update_slice.3.refs_5_) | copy-start | bytes 3076

commit v3 on v2

--- a/solution.py
+++ b/solution.py
@@ -6,7 +6,8 @@
 from jax.sharding import PartitionSpec as P
 
 ITERS = 3
-HIGH = lax.Precision.HIGHEST
+HIGHEST = lax.Precision.HIGHEST
+HIGH = lax.Precision.HIGH
 MESH = pl.DeviceIdType.MESH
 F32, BF16, I32 = jnp.float32, jnp.bfloat16, jnp.int32
 VMEM = pl.BlockSpec(memory_space=pltpu.VMEM)
@@ -56,7 +57,10 @@
             return carry
 
         lax.fori_loop(1, count, one, 0)
-    pl.semaphore_wait(barrier, sum(count - 1 for _, count in groups))
+
+
+def await_greetings(groups):
+    pl.semaphore_wait(pltpu.get_barrier_semaphore(), sum(count - 1 for _, count in groups))
 
 
 def send_all(axis, count, pick, landing, sems):
@@ -83,10 +87,10 @@
     pltpu.make_async_copy(whole, whole, sems.at[0]).wait()
 
 
-def sum_slots(count, landing):
-    total = landing[0]
+def sum_slots(count, landing, wide=None):
+    total = landing[0, :, 0:wide]
     for slot in range(1, count):
-        total = total + landing[slot]
+        total = total + landing[slot, :, 0:wide]
     return total
 
 
@@ -100,38 +104,55 @@
 
 def eliminate(work, first, last):
     size = work.shape[0]
+    steps = size // 8
     row_at = lax.broadcasted_iota(I32, (8, 1), 0)
 
-    def block(step, carry):
-        at = pl.ds(pl.multiple_of(step * 8, 8), 8)
-        panel = work[at, :]
+    def rows(step):
+        return pl.ds(pl.multiple_of(step * 8, 8), 8)
+
+    def reduce(panel):
+        columns = [jnp.broadcast_to(panel[:, j : j + 1], (8, size)) for j in range(8)]
+        left, right = panel[:, 0:size], panel[:, size:]
         for k in range(8):
-            row = panel[k : k + 1, :]
-            row = row * (1.0 / row[:, k : k + 1])
-            panel = jnp.where(row_at == k, row, panel - panel[:, k : k + 1] * row)
-        full = work[...]
-        left, right = full[:, 0:size], full[:, size:]
+            column = columns[k]
+            inverse = 1.0 / column[k : k + 1, :]
+
+            def clear(values, k=k, column=column, inverse=inverse):
+                row = values[k : k + 1, :] * inverse
+                return jnp.where(row_at == k, row, values - column * row)
+
+            for j in range(k + 1, 8):
+                columns[j] = clear(columns[j])
+            left, right = clear(left), clear(right)
+        return jnp.concatenate([left, right], axis=1)
+
+    def less(values, panel):
+        out = values
         for k in range(8):
-            column = full[:, k : k + 1]
-            left = left - column * panel[k : k + 1, 0:size]
-            right = right - column * panel[k : k + 1, size:]
-        work[:, 0:size] = pltpu.roll(left, size - 8, 1)
-        work[:, size:] = right
-        work[at, 0:size] = pltpu.roll(panel[:, 0:size], size - 8, 1)
-        work[at, size:] = panel[:, size:]
-        return carry
-
-    lax.fori_loop(first, last, block, 0)
+            out = out - values[:, k : k + 1] * panel[k : k + 1, :]
+        return out
+
+    def rolled(values):
+        return jnp.concatenate([pltpu.roll(values[:, 0:size], size - 8, 1), values[:, size:]], axis=1)
+
+    def block(step, panel):
+        following = rows(jnp.minimum(step + 1, steps - 1))
+        upcoming = reduce(rolled(less(work[following, :], panel)))
+        work[...] = rolled(less(work[...], panel))
+        work[rows(step), :] = rolled(panel)
+        return upcoming
+
+    lax.fori_loop(first, last, block, reduce(work[rows(first), :]))
 
 
 def body(
     n_sub, n_coarse,
-    operator, coupling, coarse_rows, loads, lists, maps,
+    operator_there, coupling, coarse_rows, loads, lists, maps,
     solution, residual,
-    hot, spread, pick, inverse, near, direction, rounded, product, image, pieces,
+    operator, hot, spread, pick, inverse, near, direction, rounded, product, image, pieces,
     face_out, face_in, invd, scaled, gram, blend, picked, terms_mine,
     terms, terms_in, part_rows, part_in, solved_rows, solved_in, picks, picks_in,
-    sums, sums_in, mid_rows, mid_in, sums_out, maps_in, solver, inverter, sems, face_sems,
+    sums, sums_in, mid_rows, rows_in, mid_in, sums_out, maps_in, solver, inverter, sems, face_sems, load_sem,
 ):
     me, group = lax.axis_index("sub"), lax.axis_index("coarse")
     height, width = loads.shape
@@ -192,27 +213,76 @@
 
         loop(width // TILE, one)
 
-    def all_sum_start():
-        sums_in[me] = sums[me]
-        send_all("sub", n_sub, lambda peer: sums.at[peer], sums_in, sems.at[4])
-
-    def all_sum_finish():
-        wait_all(n_sub, sums_in, sems.at[4])
-        partial = sum_slots(n_sub, sums_in)
-        mid_rows[...] = partial
-        mid_in[group] = partial
-        send_all("coarse", n_coarse, lambda peer: mid_rows, mid_in, sems.at[5])
-        wait_all(n_coarse, mid_in, sems.at[5])
-        total = sum_slots(n_coarse, mid_in)
-        mid_rows[...] = total
-        sums_out[me] = total
-        send_all("sub", n_sub, lambda peer: mid_rows, sums_out, sems.at[6])
-        wait_all(n_sub, sums_out, sems.at[6])
+    per = height // row_length
+
+    def part_of(index):
+        return pl.ds(pl.multiple_of(index * per, per), per)
+
+    def sum_parts(count, landing, wide):
+        total = landing[0:per, 0:wide]
+        for slot in range(1, count):
+            total = total + landing[slot * per : (slot + 1) * per, 0:wide]
+        return total
+
+    def send_group(count, own, device, source, landing, sem, wide):
+        def one(step, carry):
+            peer = lax.rem(own + step, count)
+            pltpu.make_async_remote_copy(
+                src_ref=source(peer),
+                dst_ref=landing.at[part_of(own), pl.ds(0, wide)],
+                send_sem=sem.at[0],
+                recv_sem=sem.at[1],
+                device_id=device(peer),
+                device_id_type=MESH,
+            ).start()
+            return carry
+
+        lax.fori_loop(1, count, one, 0)
+
+    def wait_group(count, landing, sem, wide):
+        whole = landing.at[pl.ds(0, (count - 1) * per), pl.ds(0, wide)]
+        pltpu.make_async_copy(whole, whole, sem.at[1]).wait()
+        pltpu.make_async_copy(whole, whole, sem.at[0]).wait()
+
+    def in_row(peer):
+        return {"sub": row * row_length + peer}
+
+    def in_column(peer):
+        return {"sub": peer * row_length + column}
+
+    def in_groups(peer):
+        return {"coarse": peer}
+
+    def all_sum_start(wide):
+        sums_in[part_of(column), 0:wide] = sums[part_of(column), 0:wide]
+        source = lambda peer: sums.at[part_of(peer), pl.ds(0, wide)]
+        send_group(row_length, column, in_row, source, sums_in, sems.at[4], wide)
+
+    def all_sum_finish(wide):
+        wait_group(row_length, sums_in, sems.at[4], wide)
+        total = sum_parts(row_length, sums_in, wide)
+        stages = (
+            (4, row, in_column, rows_in, sems.at[8]),
+            (n_coarse, group, in_groups, mid_in, sems.at[5]),
+        )
+        for stage, (count, own, device, landing, sem) in enumerate(stages):
+            mid_rows[stage, :, 0:wide] = total
+            landing[part_of(own), 0:wide] = total
+            source = lambda peer, stage=stage: mid_rows.at[stage, :, pl.ds(0, wide)]
+            send_group(count, own, device, source, landing, sem, wide)
+            wait_group(count, landing, sem, wide)
+            total = sum_parts(count, landing, wide)
+        mid_rows[2, :, 0:wide] = total
+        sums_out[part_of(column), 0:wide] = total
+        source = lambda peer: mid_rows.at[2, :, pl.ds(0, wide)]
+        send_group(row_length, column, in_row, source, sums_out, sems.at[6], wide)
+        wait_group(row_length, sums_out, sems.at[6], wide)
 
     face_in[...] = jnp.zeros_like(face_in)
     greet((("sub", n_sub), ("coarse", n_coarse)))
+    load = pltpu.make_async_copy(operator_there, operator, load_sem)
+    load.start()
     maps_in[me] = maps[...]
-    send_all("sub", n_sub, lambda peer: maps, maps_in, sems.at[7])
 
     def build_hot(step):
         at = lanes(step, LANES)
@@ -225,6 +295,12 @@
     )
     face_rows = height + 8 + corners
     image[...] = jnp.zeros_like(image)
+    rows_of = coarse_rows.shape[0]
+    first, rest = high_and_rest(coarse_rows[...])
+    inverse[...] = jnp.zeros_like(inverse)
+    inverse[0:rows_of, :] = first.astype(BF16)
+    inverse[256 : 256 + rows_of, :] = rest.astype(BF16)
+    load.wait()
     for at in range(0, width, LANES):
         block = operator[at : at + LANES, at : at + LANES].astype(F32)
         image[0:1, at : at + LANES] = jnp.sum(jnp.where(eye, block, 0.0), axis=0, keepdims=True)
@@ -233,12 +309,9 @@
     pieces[0:face_rows, :] = first.astype(BF16)
     pieces[face_rows : 2 * face_rows, :] = rest.astype(BF16)
     gather(face_rows)
+    await_greetings((("sub", n_sub), ("coarse", n_coarse)))
     faces_start(face_rows)
-    rows_of = coarse_rows.shape[0]
-    first, rest = high_and_rest(coarse_rows[...])
-    inverse[...] = jnp.zeros_like(inverse)
-    inverse[0:rows_of, :] = first.astype(BF16)
-    inverse[256 : 256 + rows_of, :] = rest.astype(BF16)
+    send_all("sub", n_sub, lambda peer: maps, maps_in, sems.at[7])
     wait_all(n_sub, maps_in, sems.at[7])
     for t in range(tiles):
         both = sum_slots(4, maps_in.at[pl.ds(4 * t, 4)])
@@ -283,14 +356,13 @@
     loop(width // TILE, build_weight)
     scatter_rows(rows, finish_setup)
     scaled[...] = scaled[...] * invd[...]
-    start = nt(residual[...] * scaled[...], residual[...], HIGH)
-    sums[...] = jnp.zeros_like(sums)
+    start = nt(residual[...] * scaled[...], residual[...], HIGHEST)
     for p in range(n_sub):
-        sums[p, :, 0:LANES] = start[4 * p : 4 * p + 4, :]
-    all_sum_start()
-    all_sum_finish()
-    for p in range(n_sub):
-        gram[4 * p : 4 * p + 4, :] = sums_out[p, :, 0:LANES]
+        part = slice(4 * p, 4 * p + 4)
+        sums[part, 0:LANES] = start[part, :]
+    all_sum_start(LANES)
+    all_sum_finish(LANES)
+    gram[...] = sums_out[:, 0:LANES]
 
     lane_at = lax.broadcasted_iota(I32, (8, LANES), 1)
     own_lanes = lax.broadcasted_iota(I32, (height, LANES), 1) < corners
@@ -384,20 +456,29 @@
             image[:, at] = image[:, at] + full[0:height] + full[height : 2 * height]
 
         loop(width // TILE, add_corners)
-        weighted = image[...] * scaled[...]
-        mixed = nt(weighted, residual[...], HIGH)
-        square = nt(weighted, image[...], HIGH)
         for p in range(n_sub):
             part = slice(4 * p, 4 * p + 4)
-            sums[p, :, 0:LANES] = curvature[part, :]
-            sums[p, :, LANES : 2 * LANES] = mixed[part, :]
-            sums[p, :, 2 * LANES : 3 * LANES] = square[part, :]
-        all_sum_start()
-        eliminate(inverter, 8, 16)
-        all_sum_finish()
-        for p in range(n_sub):
-            part = slice(4 * p, 4 * p + 4)
-            solver[part, 0:LANES] = sums_out[p, :, 0:LANES]
+            sums[part, 0:LANES] = curvature[part, :]
+
+        @pl.when(turn < ITERS - 1)
+        def _():
+            weighted = image[...] * scaled[...]
+            mixed = nt(weighted, residual[...], HIGH)
+            square = nt(weighted, image[...], HIGH)
+            for p in range(n_sub):
+                part = slice(4 * p, 4 * p + 4)
+                sums[part, LANES : 2 * LANES] = mixed[part, :]
+                sums[part, 2 * LANES :] = square[part, :]
+            all_sum_start(3 * LANES)
+            eliminate(inverter, 8, 16)
+            all_sum_finish(3 * LANES)
+
+        @pl.when(turn == ITERS - 1)
+        def _():
+            all_sum_start(LANES)
+            all_sum_finish(LANES)
+
+        solver[:, 0:LANES] = sums_out[:, 0:LANES]
         solver[:, height:] = gram[...]
         eliminate(solver, 0, height // 8)
         step_size = solver[:, height:]
@@ -405,13 +486,10 @@
 
         @pl.when(turn < ITERS - 1)
         def _():
-            for p in range(n_sub):
-                part = slice(4 * p, 4 * p + 4)
-                solver[part, :] = sums_out[p, :, LANES : 3 * LANES]
-            cross = nn(step_turned, solver[:, 0:LANES], HIGH)
-            twice = nn(step_turned, nn(solver[:, LANES:], step_size, HIGH), HIGH)
+            cross = nn(step_turned, sums_out[:, LANES : 2 * LANES], HIGHEST)
+            twice = nn(step_turned, nn(sums_out[:, 2 * LANES :], step_size, HIGHEST), HIGHEST)
             fresh = gram[...] - cross - cross.T + twice
-            blend[...] = nn(fresh, inverter[:, height:], HIGH)
+            blend[...] = nn(fresh, inverter[:, height:], HIGHEST)
             gram[...] = fresh
 
         factors = jnp.concatenate([step_turned, blend[...]], axis=0)
@@ -455,6 +533,7 @@
     result = [jax.ShapeDtypeStruct((height, width), F32)] * 2
     per = height // n_sub
     scratch = [
+        pltpu.VMEM((width, width), BF16),
         pltpu.VMEM((width, slots), BF16),
         pltpu.VMEM((coarse_total, split), BF16),
         pltpu.VMEM((n_coarse * 256, split), BF16),
@@ -481,21 +560,23 @@
         pltpu.VMEM((n_coarse, per, 256), F32),
         pltpu.VMEM((n_sub, per, LANES), F32),
         pltpu.VMEM((n_sub, per, LANES), F32),
-        pltpu.VMEM((n_sub, per, 3 * height), F32),
-        pltpu.VMEM((n_sub, per, 3 * height), F32),
-        pltpu.VMEM((per, 3 * height), F32),
-        pltpu.VMEM((n_coarse, per, 3 * height), F32),
-        pltpu.VMEM((n_sub, per, 3 * height), F32),
+        pltpu.VMEM((8 * (height // 8), 3 * height), F32),
+        pltpu.VMEM((8 * (height // 8), 3 * height), F32),
+        pltpu.VMEM((3, height // 8, 3 * height), F32),
+        pltpu.VMEM((4 * (height // 8), 3 * height), F32),
+        pltpu.VMEM((n_coarse * (height // 8), 3 * height), F32),
+        pltpu.VMEM((8 * (height // 8), 3 * height), F32),
         pltpu.VMEM((n_sub, 2, LANES), I32),
         pltpu.VMEM((height, 2 * height), F32),
         pltpu.VMEM((height, 2 * height), F32),
-        pltpu.SemaphoreType.DMA((8, 2)),
+        pltpu.SemaphoreType.DMA((9, 2)),
         pltpu.SemaphoreType.DMA((2, 4)),
+        pltpu.SemaphoreType.DMA,
     ]
     solved, left = pl.pallas_call(
         lambda *refs: body(n_sub, n_coarse, *refs),
         out_shape=result,
-        in_specs=[VMEM] * 6,
+        in_specs=[pl.BlockSpec(memory_space=pl.ANY)] + [VMEM] * 5,
         out_specs=[VMEM] * 2,
         scratch_shapes=scratch,
         compiler_params=pltpu.CompilerParams(

time: 265 us -> 236 us (0.89)
  Pallas kernels: 255 us -> 225 us
    pallas_call x1, Pallas kernels: 255 us -> 225 us  [local(): pl.pallas_call(lambda *refs: body(n_sub, n_coarse, *refs), out_shape=resu...]
where the time goes in v3:
time: 236 us; the launch traced here: 235 us
  Pallas kernels  225 us (95%)
  local copies, waits for them, and re-layouts  5.46 us (2%)
  other arithmetic  4.25 us (2%)
    pallas_call x1, Pallas kernels, local(): pl.pallas_call(lambda *refs: body(n_sub, n_coarse, *refs), out_shape=resu...  225 us
    unnamed x6, local copies, waits for them, and re-layouts  5.31 us

profile of v3, /device:TPU:1, one launch (start us, length us, event | category | flops | bytes accessed | tf_op | source)
XLA Modules:
  0.0 235.3 jit_solution(17537584625029809252)
XLA Ops:
  0.6 0.7 fusion.1
  1.3 0.7 add_add_fusion
  2.0 0.1 dynamic_update_slice.3.refs_5_
  2.1 0.0 copy-start
  2.1 0.7 fusion
  2.9 0.7 copy.10
  3.6 0.6 broadcast_select_fusion.refs_4_
  4.2 1.6 bitcast_convert_fusion.refs_1_
  5.8 0.0 copy-done
  5.8 224.9 %shard_map.86 = (f32[128,2048]{1,0:T(8,128)}, f32[128,2048]{1,0:T(8,128)}) custom-call(bf16[2048,2048]{1,0:T(8,128)(2,1)} %bitcast.14, f32[24,2048]{1,0:T(8,128)} %bitcast_convert_fusion.refs_1_, f32[192,1536]{1,0:T(8,128)} %refs_2_.1, f32[128,2048]{1,0:T(8,128)} %bitcast.15, s32[1,1536]{1,0:T(1,128)} %broadcast_select_fusion.refs_4_, s32[2,128]{1,0:T(2,128)} %copy-done), custom_call_target="tpu_custom_call" | custom-call | tf_op jit(solution)/shard_map/pallas_call | solution.py:576
  230.7 2.3 copy.14
  233.0 2.3 copy.15
  (2 shorter events, 0.0 us)
Async XLA Ops:
  2.1 3.6 %copy-start = (s32[2,128]{1,0:T(2,128)}, s32[2,128]{1,0:T(2,128)S(1)}, u32[]{:S(2)}) copy-start(s32[2,128]{1,0:T(2,128)S(1)} %dynamic_update_slice.3.refs_5_) | copy-start | bytes 3076

commit v4 on v3

--- a/solution.py
+++ b/solution.py
@@ -258,25 +258,35 @@
         source = lambda peer: sums.at[part_of(peer), pl.ds(0, wide)]
         send_group(row_length, column, in_row, source, sums_in, sems.at[4], wide)
 
-    def all_sum_finish(wide):
+    def all_sum_stage(stage, count, own, device, landing, sem, total, wide):
+        mid_rows[stage, :, 0:wide] = total
+        landing[part_of(own), 0:wide] = total
+        source = lambda peer: mid_rows.at[stage, :, pl.ds(0, wide)]
+        send_group(count, own, device, source, landing, sem, wide)
+
+    def all_sum_rows(wide):
         wait_group(row_length, sums_in, sems.at[4], wide)
         total = sum_parts(row_length, sums_in, wide)
-        stages = (
-            (4, row, in_column, rows_in, sems.at[8]),
-            (n_coarse, group, in_groups, mid_in, sems.at[5]),
-        )
-        for stage, (count, own, device, landing, sem) in enumerate(stages):
-            mid_rows[stage, :, 0:wide] = total
-            landing[part_of(own), 0:wide] = total
-            source = lambda peer, stage=stage: mid_rows.at[stage, :, pl.ds(0, wide)]
-            send_group(count, own, device, source, landing, sem, wide)
-            wait_group(count, landing, sem, wide)
-            total = sum_parts(count, landing, wide)
-        mid_rows[2, :, 0:wide] = total
-        sums_out[part_of(column), 0:wide] = total
-        source = lambda peer: mid_rows.at[2, :, pl.ds(0, wide)]
-        send_group(row_length, column, in_row, source, sums_out, sems.at[6], wide)
+        all_sum_stage(0, 4, row, in_column, rows_in, sems.at[8], total, wide)
+
+    def all_sum_groups(wide):
+        wait_group(4, rows_in, sems.at[8], wide)
+        total = sum_parts(4, rows_in, wide)
+        all_sum_stage(1, n_coarse, group, in_groups, mid_in, sems.at[5], total, wide)
+
+    def all_sum_back(wide):
+        wait_group(n_coarse, mid_in, sems.at[5], wide)
+        total = sum_parts(n_coarse, mid_in, wide)
+        all_sum_stage(2, row_length, column, in_row, sums_out, sems.at[6], total, wide)
+
+    def all_sum_end(wide):
         wait_group(row_length, sums_out, sems.at[6], wide)
+
+    def all_sum_finish(wide):
+        all_sum_rows(wide)
+        all_sum_groups(wide)
+        all_sum_back(wide)
+        all_sum_end(wide)
 
     face_in[...] = jnp.zeros_like(face_in)
     greet((("sub", n_sub), ("coarse", n_coarse)))
@@ -320,6 +330,13 @@
         spread[:, at] = jnp.where(index == both[0:1, :], 1.0, 0.0).astype(BF16)
         index = lax.broadcasted_iota(I32, (pick.shape[0], LANES), 0) + 1
         pick[:, at] = jnp.where(index == both[1:2, :], 1.0, 0.0).astype(BF16)
+    ones = jnp.ones((16, slots), BF16)
+
+    def build_weight(step):
+        at = lanes(step, TILE)
+        scaled[:, at] = 1.0 / (1.0 + nt(ones, hot[at, :])[0:1])
+
+    loop(width // TILE, build_weight)
     faces_wait(face_rows)
 
     product[...] = jnp.zeros_like(product)
@@ -347,13 +364,6 @@
         rounded[:, at] = direction[:, at].astype(BF16)
         solution[:, at] = jnp.zeros_like(combined)
 
-    ones = jnp.ones((16, slots), BF16)
-
-    def build_weight(step):
-        at = lanes(step, TILE)
-        scaled[:, at] = 1.0 / (1.0 + nt(ones, hot[at, :])[0:1])
-
-    loop(width // TILE, build_weight)
     scatter_rows(rows, finish_setup)
     scaled[...] = scaled[...] * invd[...]
     start = nt(residual[...] * scaled[...], residual[...], HIGHEST)
@@ -361,8 +371,6 @@
         part = slice(4 * p, 4 * p + 4)
         sums[part, 0:LANES] = start[part, :]
     all_sum_start(LANES)
-    all_sum_finish(LANES)
-    gram[...] = sums_out[:, 0:LANES]
 
     lane_at = lax.broadcasted_iota(I32, (8, LANES), 1)
     own_lanes = lax.broadcasted_iota(I32, (height, LANES), 1) < corners
@@ -388,6 +396,11 @@
             pieces[height : 2 * height, at] = rest.astype(BF16)
 
         loop(width // TILE, multiply)
+
+        @pl.when(turn == 0)
+        def _():
+            all_sum_rows(LANES)
+
         wait_all(n_sub, terms_in, sems.at[0])
         row_tiles = [sum_slots(4, terms_in.at[pl.ds(4 * t, 4)]) for t in range(tiles)]
         partial = stacked_dot(jnp.concatenate(row_tiles, axis=1), spread[...], nt)
@@ -396,7 +409,17 @@
         send_all("coarse", n_coarse, lambda peer: part_rows, part_in, sems.at[1])
         gather(height)
         faces_start(height)
+
+        @pl.when(turn == 0)
+        def _():
+            all_sum_groups(LANES)
+
         wait_all(n_coarse, part_in, sems.at[1])
+
+        @pl.when(turn == 0)
+        def _():
+            all_sum_back(LANES)
+
         wide = stacked_dot(sum_slots(n_coarse, part_in), inverse[...], nt)
         solved = wide[:, 0:256] + wide[:, 256:512]
         solved_rows[...] = solved
@@ -404,9 +427,16 @@
         send_all("coarse", n_coarse, lambda peer: solved_rows, solved_in, sems.at[2])
         both = nt(rounded[...], pieces[0 : 2 * height, :])
         curvature = both[:, 0:height] + both[:, height : 2 * height]
-        inverter[:, 0:height] = gram[...]
-        inverter[:, height:] = jnp.where(eye, 1.0, 0.0)
-        eliminate(inverter, 0, 4)
+
+        def begin_inverse():
+            inverter[:, 0:height] = gram[...]
+            inverter[:, height:] = jnp.where(eye, 1.0, 0.0)
+
+        @pl.when(turn > 0)
+        def _():
+            begin_inverse()
+            eliminate(inverter, 0, 4)
+
         wait_all(n_coarse, solved_in, sems.at[2])
         everything = jnp.concatenate([solved_in[c] for c in range(n_coarse)], axis=1)
         chosen = stacked_dot(everything, pick[...], nn)
@@ -440,7 +470,18 @@
             image[:, at] = product[:, at] + added
 
         scatter_rows(height, add_faces)
-        eliminate(inverter, 4, 8)
+
+        @pl.when(turn > 0)
+        def _():
+            eliminate(inverter, 4, 8)
+
+        @pl.when(turn == 0)
+        def _():
+            all_sum_end(LANES)
+            gram[...] = sums_out[:, 0:LANES]
+            begin_inverse()
+            eliminate(inverter, 0, 4)
+
         wait_all(n_sub, picks_in, sems.at[3])
         for p in range(n_sub):
             picked[4 * p : 4 * p + 4, :] = picks_in[p]
@@ -470,7 +511,7 @@
                 sums[part, LANES : 2 * LANES] = mixed[part, :]
                 sums[part, 2 * LANES :] = square[part, :]
             all_sum_start(3 * LANES)
-            eliminate(inverter, 8, 16)
+            eliminate(inverter, jnp.where(turn == 0, 4, 8), 16)
             all_sum_finish(3 * LANES)
 
         @pl.when(turn == ITERS - 1)
@@ -508,6 +549,11 @@
 
     blend[...] = jnp.zeros_like(blend)
     loop(ITERS, iteration)
+
+
+def hand_on(solved, left, solved_out, left_out):
+    solved_out[...] = solved[...]
+    left_out[...] = left[...]
 
 
 def local(
@@ -583,6 +629,9 @@
             collective_id=0, has_side_effects=True, vmem_limit_bytes=60 << 20
         ),
     )(local_operators[0], couplings[0].astype(F32), coarse_inverse, local_loads[0], marked, maps)
+    solved, left = pl.pallas_call(
+        hand_on, out_shape=result, in_specs=[VMEM] * 2, out_specs=[VMEM] * 2
+    )(solved, left)
     return (solved[None], left[None])
 
 

time: 236 us -> 218 us (0.924)
  Pallas kernels: 225 us -> 212 us
  local copies, waits for them, and re-layouts: 5.46 us -> 0.87 us
    pallas_call x1, Pallas kernels: 225 us -> 209 us  [local(): pl.pallas_call(lambda *refs: body(n_sub, n_coarse, *refs), out_shape=resu...]
    unnamed x6 -> x4, local copies, waits for them, and re-layouts: 5.31 us -> 0.72 us
    pallas_call x0 -> x1, Pallas kernels: none -> 2.93 us  [local(): pl.pallas_call(hand_on, out_shape=result, in_specs=[VMEM] * 2, out_specs=...]
where the time goes in v4:
time: 218 us
  Pallas kernels  212 us (97%)
  other arithmetic  4.25 us (2%)
    pallas_call x1, Pallas kernels, local(): pl.pallas_call(lambda *refs: body(n_sub, n_coarse, *refs), out_shape=resu...  209 us

profile of v4, /device:TPU:1, one launch (start us, length us, event | category | flops | bytes accessed | tf_op | source)
XLA Modules:
  0.0 218.1 jit_solution(126185766717947051)
XLA Ops:
  0.6 0.7 fusion.1
  1.3 0.7 add_add_fusion
  2.0 0.1 dynamic_update_slice.3.refs_5_
  2.1 0.0 copy-start
  2.1 0.7 fusion
  2.9 0.7 copy.10
  3.6 0.6 broadcast_select_fusion.refs_4_
  4.2 1.6 bitcast_convert_fusion.refs_1_
  5.8 0.0 copy-done
  5.8 209.4 %shard_map.86 = (f32[128,2048]{1,0:T(8,128)}, f32[128,2048]{1,0:T(8,128)}) custom-call(bf16[2048,2048]{1,0:T(8,128)(2,1)} %bitcast.14, f32[24,2048]{1,0:T(8,128)} %bitcast_convert_fusion.refs_1_, f32[192,1536]{1,0:T(8,128)} %refs_2_.1, f32[128,2048]{1,0:T(8,128)} %bitcast.15, s32[1,1536]{1,0:T(1,128)} %broadcast_select_fusion.refs_4_, s32[2,128]{1,0:T(2,128)} %copy-done), custom_call_target="tpu_custom_call" | custom-call | tf_op jit(solution)/shard_map/pallas_call | solution.py:622
  215.2 2.9 %shard_map.87 = (f32[128,2048]{1,0:T(8,128)}, f32[128,2048]{1,0:T(8,128)}) custom-call(f32[128,2048]{1,0:T(8,128)} %get-tuple-element.6.solved, f32[128,2048]{1,0:T(8,128)} %get-tuple-element.7.left), custom_call_target="tpu_custom_call" | custom-call | tf_op jit(solution)/shard_map/pallas_call | solution.py:632
  (2 shorter events, 0.0 us)
Async XLA Ops:
  2.1 3.6 %copy-start = (s32[2,128]{1,0:T(2,128)}, s32[2,128]{1,0:T(2,128)S(1)}, u32[]{:S(2)}) copy-start(s32[2,128]{1,0:T(2,128)S(1)} %dynamic_update_slice.3.refs_5_) | copy-start | bytes 3076
